TPU v7x, 128 devices: a whole 4x4x4 slice. The times are simulated.
128 devices in a mesh: src: 16 (over x, z), tgt: 8 (over y, core).
Axes of the slice: x: 4, y: 4, z: 4, core: 2. Of those that a mesh axis runs over, the one named last changes fastest.
Arguments:
- source_embed: bfloat16 [32, 131072], P('tgt', 'src'), may hold values from -4 to 4
- target_embed: bfloat16 [32, 131072], P('src', 'tgt'), may hold values from -4 to 4
- target_potential: float32 [131072], P('tgt'), may hold values from -15 to 15
- log_source_mass: float32 [131072], P('src'), may hold values from -14 to -10
- log_target_mass: float32 [131072], P('tgt'), may hold values from -14 to -10
- tile_list: int32 [16, 8, 2, 64], P('src', 'tgt'), may hold values from 0 to 31, as said below
- counts: int32 [16, 8], P('src', 'tgt'), may hold values from 8 to 64, as said below
Outputs:
- row_potential: float32 [131072], P('src')
- column_potential: float32 [131072], P('tgt')
Inputs may be any that keep to these rules, and one draw needn't show every extreme that they name: `tile_list`: on device (s, t) the first counts[s, t] entries are distinct pairs; every source tile and every target tile lies in some live pair; entries past the count are valid tile numbers but not live. `counts`: some device's count is 64 in every draw.
All inputs are finite; a program needn't handle non-finite values.
Results may differ from a plain program's by a relative error of at most 0.0029.
Values may be sent and summed in bfloat16 or wider, within the bound.
No kernel may reach another device: no remote copies, remote signals or barrier semaphores. Data moves between devices by JAX's collectives and lax.ppermute only.
A program may use at most 64 MiB of HBM per device.

v0:
```python
import jax
import jax.numpy as jnp
from jax import lax
from jax.sharding import PartitionSpec as P

TILE = 512


epsilon = 0.1
lowest = -1e30


def joined(part, axis, combine):
    gathered = jax.tree.map(lambda a: lax.all_gather(a, axis), part)

    def take(source):
        return jax.tree.map(lambda a: lax.dynamic_index_in_dim(a, source, 0, False), gathered)

    return lax.fori_loop(
        1, lax.axis_size(axis), lambda source, state: combine(state, take(source)), take(0)
    )


def merge_pair(former, latter):
    highest = jnp.maximum(former[0], latter[0])
    return (
        highest,
        former[1] * jnp.exp(former[0] - highest) + latter[1] * jnp.exp(latter[0] - highest),
    )


def tile_cost(source_tile, target_tile, source_square, target_square):
    inner = jnp.dot(source_tile.T, target_tile, preferred_element_type=jnp.float32)
    return (source_square[:, None] + target_square[None, :] - 2.0 * inner) / (
        2.0 * source_tile.shape[0]
    )


def local(
    source_embed,
    target_embed,
    target_potential,
    log_source_mass,
    log_target_mass,
    tile_list,
    counts,
):
    source_full = lax.all_gather(source_embed, "tgt", axis=0, tiled=True)
    target_full = lax.all_gather(target_embed, "src", axis=0, tiled=True)
    width = source_full.shape[0]
    tile_size = TILE
    source_square = jnp.sum(jnp.square(source_full.astype(jnp.float32)), axis=0)
    target_square = jnp.sum(jnp.square(target_full.astype(jnp.float32)), axis=0)
    own_list = tile_list[0, 0]
    own_count = counts[0, 0]
    target_pair = target_full[None]
    square_pair = target_square[None]
    potential_pair = target_potential[None]
    first_step = 0

    def locate(step_at):
        return (jnp.int32(0), own_list[0, step_at], own_list[1, step_at])

    def fetch_tile(step_at):
        block_at, source_at, target_at = locate(step_at)
        source_tile = lax.dynamic_slice_in_dim(source_full, source_at * tile_size, tile_size, 1)
        target_tile = lax.dynamic_slice(
            target_pair, (block_at, 0, target_at * tile_size), (1, width, tile_size)
        )[0]
        source_part = lax.dynamic_slice_in_dim(source_square, source_at * tile_size, tile_size)
        target_part = lax.dynamic_slice(
            square_pair, (block_at, target_at * tile_size), (1, tile_size)
        )[0]
        return (
            block_at,
            source_at,
            target_at,
            tile_cost(source_tile, target_tile, source_part, target_part),
        )

    def row_step(step_at, totals):
        block_at, source_at, target_at, cost_tile = fetch_tile(step_at)
        pot_tile = lax.dynamic_slice(
            potential_pair, (block_at, target_at * tile_size), (1, tile_size)
        )[0]
        scores = (pot_tile[None, :] - cost_tile) / epsilon
        tile_max = jnp.max(scores, axis=1)
        tile_sum = jnp.sum(jnp.exp(scores - tile_max[:, None]), axis=1)
        offset = source_at * tile_size
        previous = (
            lax.dynamic_slice_in_dim(totals[0], offset, tile_size),
            lax.dynamic_slice_in_dim(totals[1], offset, tile_size),
        )
        updated = merge_pair(previous, (tile_max, tile_sum))
        return (
            lax.dynamic_update_slice_in_dim(totals[0], updated[0], offset, 0),
            lax.dynamic_update_slice_in_dim(totals[1], updated[1], offset, 0),
        )

    source_cells = source_full.shape[1]
    row_init = (
        jnp.full((source_cells,), lowest, jnp.float32),
        jnp.zeros((source_cells,), jnp.float32),
    )
    row_max, row_sum = lax.fori_loop(first_step, own_count, row_step, row_init)
    row_max, row_sum = joined((row_max, row_sum), "tgt", merge_pair)
    row_potential = epsilon * log_source_mass - epsilon * (row_max + jnp.log(row_sum))

    def col_step(step_at, totals):
        block_at, source_at, target_at, cost_tile = fetch_tile(step_at)
        pot_tile = lax.dynamic_slice_in_dim(row_potential, source_at * tile_size, tile_size)
        scores = (pot_tile[:, None] - cost_tile) / epsilon
        tile_max = jnp.max(scores, axis=0)
        tile_sum = jnp.sum(jnp.exp(scores - tile_max[None, :]), axis=0)
        corner = (block_at, target_at * tile_size)
        previous = (
            lax.dynamic_slice(totals[0], corner, (1, tile_size))[0],
            lax.dynamic_slice(totals[1], corner, (1, tile_size))[0],
        )
        updated = merge_pair(previous, (tile_max, tile_sum))
        return (
            lax.dynamic_update_slice(totals[0], updated[0][None], corner),
            lax.dynamic_update_slice(totals[1], updated[1][None], corner),
        )

    blocks = target_pair.shape[0]
    target_cells = target_full.shape[1]
    col_init = (
        jnp.full((blocks, target_cells), lowest, jnp.float32),
        jnp.zeros((blocks, target_cells), jnp.float32),
    )
    col_max, col_sum = lax.fori_loop(first_step, own_count, col_step, col_init)
    col_max, col_sum = (col_max[0], col_sum[0])
    highest = lax.pmax(col_max.astype(jnp.bfloat16), "src").astype(col_max.dtype)
    col_sum = lax.psum((col_sum * jnp.exp(col_max - highest)).astype(jnp.bfloat16), "src").astype(
        jnp.float32
    )
    col_max = highest
    column_potential = epsilon * log_target_mass - epsilon * (col_max + jnp.log(col_sum))
    return (row_potential, column_potential)


def solution(mesh):
    return jax.shard_map(
        local,
        mesh=mesh,
        in_specs=(
            P("tgt", "src"),
            P("src", "tgt"),
            P("tgt"),
            P("src"),
            P("tgt"),
            P("src", "tgt", None, None),
            P("src", "tgt"),
        ),
        out_specs=(P("src"), P("tgt")),
        check_vma=False,
    )
```

profile of v0, /device:TPU:8, one launch (start us, length us, event | category | flops | bytes accessed | tf_op | source)
XLA Modules:
  0.0 730.1 jit_solution(294852881005708144)
XLA Ops:
  7.9 13.5 %all-gather.2 = bf16[8,4,8192]{2,1,0:T(4,128)(2,1)S(1)} all-gather(bf16[1,4,8192]{2,1,0:T(4,128)(2,1)} %bitcast.64), channel_id=1, replica_groups=mesh['src'=16,'tgt'=8] {'tgt'}, dimensions={0}, use_global_device_ids=true | all-gather | bytes 589824 | tf_op jit(solution)/shard_map/all_gather | solution.py:48
  21.7 33.6 %all-gather.6.cloned.1.call-done = bf16[16,2,16384]{2,1,0:T(2,128)(2,1)} async-done(((bf16[1,2,16384]{2,1,0:T(2,128)(2,1)}), bf16[16,2,16384]{2,1,0:T(2,128)(2,1)}) %all-gather.6.cloned.1.call-update) | async-done | bytes 1048592 | tf_op jit(solution)/shard_map/all_gather | solution.py:49
  55.3 1.6 broadcast_in_dim.32
  56.9 1.2 multiply_reduce_fusion
  58.1 201.4 %while.41 = (s32[]{:T(128)}, f32[8192]{0:T(1024)S(1)}, f32[8192]{0:T(1024)S(1)}, s32[]{:T(128)}, s32[2,64]{1,0:T(2,128)S(1)}, /*index=5*/f32[1,16384]{1,0:T(1,12...) while((s32[]{:T(128)}, f32[8192]{0:T(1024)S(1)}, ...), condition=%wide.region_5.0_spmd, body=%wide.region_2.0_spmd.sunk | while | flops 19138572 | bytes 2199867 | solution.py:105
  60.0 0.7 constant_dynamic-slice_fusion.16
  64.3 0.7 constant_dynamic-slice_fusion.16
  68.6 0.7 constant_dynamic-slice_fusion.16
  72.8 0.7 constant_dynamic-slice_fusion.16
  77.1 0.7 constant_dynamic-slice_fusion.16
  81.4 0.7 constant_dynamic-slice_fusion.16
  85.7 0.7 constant_dynamic-slice_fusion.16
  89.9 0.7 constant_dynamic-slice_fusion.16
  94.2 0.7 constant_dynamic-slice_fusion.16
  98.5 0.7 constant_dynamic-slice_fusion.16
  102.7 0.7 constant_dynamic-slice_fusion.16
  107.0 0.7 constant_dynamic-slice_fusion.16
  111.3 0.7 constant_dynamic-slice_fusion.16
  115.5 0.7 constant_dynamic-slice_fusion.16
  119.8 0.7 constant_dynamic-slice_fusion.16
  124.1 0.7 constant_dynamic-slice_fusion.16
  128.4 0.7 constant_dynamic-slice_fusion.16
  132.6 0.7 constant_dynamic-slice_fusion.16
  136.9 0.7 constant_dynamic-slice_fusion.16
  141.2 0.7 constant_dynamic-slice_fusion.16
  145.5 0.7 constant_dynamic-slice_fusion.16
  149.7 0.7 constant_dynamic-slice_fusion.16
  154.0 0.7 constant_dynamic-slice_fusion.16
  158.3 0.7 constant_dynamic-slice_fusion.16
  162.5 0.7 constant_dynamic-slice_fusion.16
  166.8 0.7 constant_dynamic-slice_fusion.16
  171.1 0.7 constant_dynamic-slice_fusion.16
  175.4 0.7 constant_dynamic-slice_fusion.16
  179.6 0.7 constant_dynamic-slice_fusion.16
  183.9 0.7 constant_dynamic-slice_fusion.16
  201.0 0.7 constant_dynamic-slice_fusion.16
  209.5 0.7 constant_dynamic-slice_fusion.16
  213.8 0.7 constant_dynamic-slice_fusion.16
  222.3 0.7 constant_dynamic-slice_fusion.16
  226.6 0.7 constant_dynamic-slice_fusion.16
  230.9 0.7 constant_dynamic-slice_fusion.16
  256.5 0.7 constant_dynamic-slice_fusion.16
  259.5 81.2 %all-gather = f32[65536]{0:T(1024)S(1)} all-gather(f32[8192]{0:T(1024)S(1)} %get-tuple-element.243), channel_id=2, replica_groups=mesh['src'=16,'tgt'=8] {'tgt'}, dimensions={0}, use_global_device_ids=true | all-gather | bytes 294912 | tf_op jit(solution)/shard_map/all_gather | solution.py:14
  340.7 12.8 %all-gather.1 = f32[65536]{0:T(1024)S(1)} all-gather(f32[8192]{0:T(1024)S(1)} %get-tuple-element.244), channel_id=3, replica_groups=mesh['src'=16,'tgt'=8] {'tgt'}, dimensions={0}, use_global_device_ids=true | all-gather | bytes 294912 | tf_op jit(solution)/shard_map/all_gather | solution.py:14
  353.7 0.8 while.42
  354.6 167.2 %while.43 = (s32[]{:T(128)}, f32[1,16384]{1,0:T(1,128)S(1)}, f32[1,16384]{1,0:T(1,128)S(1)}, s32[]{:T(128)}, s32[2,64]{1,0:T(2,128)S(1)}, /*index=5*/f32[8192]{0...) while((s32[]{:T(128)}, f32[1,16384]{1,0:T(1,128)S(1)}, ...), condition=%wide.region_11.12_spmd, body=%wide.region_8.11_spmd.sunk | while | flops 19138572 | bytes 2199871 | solution.py:132
  521.9 131.2 %pmax.7 = bf16[16384]{0:T(1024)(128)(2,1)S(1)} all-reduce(bf16[16384]{0:T(1024)(128)(2,1)S(1)} %convert_element_type.20), channel_id=1, replica_groups=mesh['src'=16,'tgt'=8] {'src'}, use_global_device_ids=true, to_apply=%region_12.13 | all-reduce | flops 16384 | bytes 65536 | tf_op jit(solution)/shard_map/pmax | solution.py:134
  653.0 69.6 %psum.7 = bf16[16384]{0:T(1024)(128)(2,1)S(1)} all-reduce(bf16[16384]{0:T(1024)(128)(2,1)S(1)} %fusion.18), channel_id=1, replica_groups=mesh['src'=16,'tgt'=8] {'src'}, use_global_device_ids=true, to_apply=%region_13.14 | all-reduce | flops 16384 | bytes 65536 | tf_op jit(solution)/shard_map/psum | solution.py:135
  (614 shorter events, 156.8 us)
Async XLA Ops:
  7.2 48.1 %all-gather.6.cloned.1.call-start = ((), (), s32[]{:S(2)}) async-start(), calls=%async_computation | async-start | bytes 1114112 | tf_op jit(solution)/shard_map/all_gather | solution.py:49
  55.3 1.6 copy-start
  56.9 1.2 copy-start.1
  353.6 0.9 copy-start.4
  354.6 368.0 %copy-start.2 = (f32[16384]{0:T(1024)S(1)}, f32[16384]{0:T(1024)}, u32[]{:S(2)}) copy-start(f32[16384]{0:T(1024)} %param.17) | copy-start | bytes 196612
  521.8 201.5 %copy-start.3 = (f32[8192]{0:T(1024)}, f32[8192]{0:T(1024)S(1)}, u32[]{:S(2)}) copy-start(f32[8192]{0:T(1024)S(1)} %get-tuple-element.637) | copy-start | bytes 98308
Sparse Core Ops, SparseCore 0:
  10.1 45.1 all-gather.5
where the time goes:
time: 738 us; the launch traced here: 730 us
  blocking collectives  308 us (42%)
  loops' own time  189 us (26%)
  local copies, waits for them, and re-layouts  109 us (15%)
  matrix products  42.7 us (6%)
  waiting for transfers between devices  34.3 us (5%)
  other arithmetic  32.9 us (4%)
  between operations  14.2 us (2%)
    pmax x1, blocking collectives, local(): lax.pmax(col_max.astype(jnp.bfloat16), 'src').astype(col_max.dtype)  131 us
    another operation x1, loops' own time, local(): col_max, col_sum = lax.fori_loop(first_step, own_count, col_step, col_init)  96.6 us
    all_gather x2, blocking collectives, joined(): gathered = jax.tree.map(lambda a: lax.all_gather(a, axis), part)  94 us
    another operation x1, loops' own time, local(): row_max, row_sum = lax.fori_loop(first_step, own_count, row_step, row_init)  92.2 us
    psum x1, blocking collectives, local(): lax.psum((col_sum * jnp.exp(col_max - highest)).astype(jnp.bfloat16), 'src')  69.6 us
    dynamic_slice x94, local copies, waits for them, and re-layouts, locate(): return (jnp.int32(0), own_list[0, step_at], own_list[1, step_at])  62.9 us
    dot_general x94, matrix products, tile_cost(): jnp.dot(source_tile.T, target_tile, preferred_element_type=jnp.float32)  42.7 us
    all_gather x1, waiting for transfers between devices, local(): target_full = lax.all_gather(target_embed, 'src', axis=0, tiled=True)  33.6 us
  transfers between devices with their start and end apart: 1, of which 1 were waited for; matrix products, arithmetic and copies ran while one was open for 0% of the time, Pallas kernels for 0%

commit v1 on v0

v1 whole, which is shorter than its diff:
```python
import functools

import jax
import jax.numpy as jnp
from jax import lax
from jax.experimental import pallas as pl
from jax.experimental.pallas import tpu as pltpu
from jax.sharding import PartitionSpec as P

TILE = 512
WIDTH = 32
DEPTH = 48
EPSILON = 0.1
HALF = float(WIDTH)
UNIT = 1.0 / (EPSILON * HALF)
ALPHA = UNIT * 1.4426950408889634
LOWEST = -1e30


def scaled_exp(value):
    return jnp.exp2(value * ALPHA)


def lse_kernel(red_row, keep_row, list_ref, count_ref, red_ref, keep_ref, bias_ref, out_ref, red_rows, keep_cols, top, total):
    red_tiles = red_ref.shape[1] // TILE
    keep_tiles = keep_ref.shape[1] // TILE

    def at_tile(tile):
        return pl.ds(pl.multiple_of(tile * TILE, TILE), TILE)

    def prepare_reduced(tile, _):
        at = at_tile(tile)
        cells = red_ref[:, at].astype(jnp.float32)
        bias = HALF * bias_ref[:, at] - 0.5 * jnp.sum(cells * cells, axis=0, keepdims=True)
        first = bias.astype(jnp.bfloat16).astype(jnp.float32)
        rest = bias - first
        second = rest.astype(jnp.bfloat16).astype(jnp.float32)
        filler = jnp.zeros((128 - WIDTH - 3, TILE), jnp.float32)
        rows = jnp.concatenate([cells, first, second, rest - second, filler], axis=0)
        red_rows[at, :] = jnp.transpose(rows).astype(jnp.bfloat16)
        return 0

    def prepare_kept(tile, _):
        at = at_tile(tile)
        keep_cols[0:WIDTH, at] = keep_ref[:, at]
        rows = lax.broadcasted_iota(jnp.int32, (DEPTH - WIDTH, TILE), 0)
        keep_cols[WIDTH:DEPTH, at] = jnp.where(rows < 3, 1.0, 0.0).astype(jnp.bfloat16)
        top[:, at] = jnp.full((8, TILE), LOWEST, jnp.float32)
        total[:, at] = jnp.zeros((8, TILE), jnp.float32)
        return 0

    lax.fori_loop(0, red_tiles, prepare_reduced, 0)
    lax.fori_loop(0, keep_tiles, prepare_kept, 0)

    lanes_of, rows_of = 256, 128

    def step(entry, _):
        red_at = pl.multiple_of(list_ref[red_row, entry] * TILE, TILE)
        keep_at = pl.multiple_of(list_ref[keep_row, entry] * TILE, TILE)
        for lane in range(0, TILE, lanes_of):
            lanes = pl.ds(pl.multiple_of(keep_at + lane, lanes_of), lanes_of)
            highest, summed = top[:, lanes], total[:, lanes]
            columns = keep_cols[:, lanes]
            for row in range(0, TILE, rows_of):
                block = red_rows[pl.ds(pl.multiple_of(red_at + row, rows_of), rows_of), :DEPTH]
                z = jnp.dot(block, columns, preferred_element_type=jnp.float32)
                z = z.reshape(rows_of // 8, 8, lanes_of)
                higher = jnp.maximum(highest, jnp.max(z, axis=0))
                summed = summed * scaled_exp(highest - higher) + jnp.sum(scaled_exp(z - higher[None]), axis=0)
                highest = higher
            top[:, lanes] = highest
            total[:, lanes] = summed
        return 0

    lax.fori_loop(0, count_ref[0, 0], step, 0)

    def finish(tile, _):
        at = at_tile(tile)
        highest = jnp.max(top[:, at], axis=0, keepdims=True)
        summed = jnp.sum(total[:, at] * scaled_exp(top[:, at] - highest), axis=0, keepdims=True)
        cells = keep_ref[:, at].astype(jnp.float32)
        half_square = 0.5 * jnp.sum(cells * cells, axis=0, keepdims=True)
        out_ref[:, at] = highest + jnp.log(jnp.maximum(summed, 1.0)) * (1.0 / UNIT) - half_square
        return 0

    lax.fori_loop(0, keep_tiles, finish, 0)


def block_lse(name, red_row, reduced, kept, bias, own_list, own_count):
    red_cells, keep_cells = reduced.shape[1], kept.shape[1]
    vmem = pl.BlockSpec(memory_space=pltpu.VMEM)
    smem = pl.BlockSpec(memory_space=pltpu.SMEM)
    return pl.pallas_call(
        functools.partial(lse_kernel, red_row, 1 - red_row),
        name=name,
        out_shape=jax.ShapeDtypeStruct((1, keep_cells), jnp.float32),
        in_specs=[smem, smem, vmem, vmem, vmem],
        out_specs=vmem,
        scratch_shapes=[
            pltpu.VMEM((red_cells, 128), jnp.bfloat16),
            pltpu.VMEM((DEPTH, keep_cells), jnp.bfloat16),
            pltpu.VMEM((8, keep_cells), jnp.float32),
            pltpu.VMEM((8, keep_cells), jnp.float32),
        ],
        compiler_params=pltpu.CompilerParams(vmem_limit_bytes=32 << 20),
    )(own_list, own_count, reduced, kept, bias)


def merged(parts):
    highest = functools.reduce(jnp.maximum, parts)
    summed = sum(jnp.exp(UNIT * (part - highest)) for part in parts)
    return highest + jnp.log(summed) * (1.0 / UNIT)


def along(axis, size, group, stride, shift):
    pairs = []
    for index in range(size):
        digit = index // stride % group
        pairs.append((index, index + ((digit + shift) % group - digit) * stride))
    return lambda value: lax.ppermute(value, axis, pairs)


def local(source_embed, target_embed, target_potential, log_source_mass, log_target_mass, tile_list, counts):
    sources = lax.axis_size("src")
    copies = jnp.broadcast_to(target_embed[None], (sources,) + target_embed.shape)
    target_full = lax.all_to_all(copies, "src", 0, 0).reshape(WIDTH, -1)
    source_full = lax.all_gather(source_embed, "tgt", axis=0, tiled=True)
    own_list = tile_list[0, 0]

    row = block_lse("row_lse", 1, target_full, source_full, target_potential[None], own_list, counts)
    row = merged([row, along("tgt", 8, 2, 1, 1)(row)])
    row = merged([row] + [along("tgt", 8, 4, 2, shift)(row) for shift in (1, 2, 3)])
    row_potential = EPSILON * log_source_mass[None] - row * (1.0 / HALF)

    column = block_lse("column_lse", 0, source_full, target_full, row_potential, own_list, counts)
    column = merged([column] + [along("src", 16, 4, 4, shift)(column) for shift in (1, 2, 3)])
    column = merged([column] + [along("src", 16, 4, 1, shift)(column) for shift in (1, 2, 3)])
    column_potential = EPSILON * log_target_mass[None] - column * (1.0 / HALF)
    return row_potential[0], column_potential[0]


def solution(mesh):
    return jax.shard_map(
        local,
        mesh=mesh,
        in_specs=(
            P("tgt", "src"),
            P("src", "tgt"),
            P("tgt"),
            P("src"),
            P("tgt"),
            P("src", "tgt", None, None),
            P("src", "tgt"),
        ),
        out_specs=(P("src"), P("tgt")),
        check_vma=False,
    )
```

time: 738 us -> 111 us (0.15)
  the two profiles are of different devices: /device:TPU:8 before, /device:TPU:0 now
where the time goes in v1:
time: 111 us
  starting transfers between devices  60.6 us (55%)
  Pallas kernels  16 us (14%)
  blocking collectives  13.6 us (12%)
  waiting for transfers between devices  13.5 us (12%)
  local copies, waits for them, and re-layouts  3.86 us (3%)
  other arithmetic  1.98 us (2%)
  between operations  1.42 us (1%)
    ppermute x10, starting transfers between devices, along(): return lambda value: lax.ppermute(value, axis, pairs)  52.5 us
    pallas_call x2, Pallas kernels, block_lse(): pl.pallas_call(functools.partial(lse_kernel, red_row, 1 - red_row), name=...  16 us
    all_gather x1, blocking collectives, local(): source_full = lax.all_gather(source_embed, 'tgt', axis=0, tiled=True)  13.6 us
    ppermute x10, waiting for transfers between devices, along(): return lambda value: lax.ppermute(value, axis, pairs)  10.2 us
    all_to_all x1, starting transfers between devices, local(): target_full = lax.all_to_all(copies, 'src', 0, 0).reshape(WIDTH, -1)  8.09 us
    all_to_all x1, waiting for transfers between devices, local(): target_full = lax.all_to_all(copies, 'src', 0, 0).reshape(WIDTH, -1)  3.27 us
    broadcast_in_dim x1, local copies, waits for them, and re-layouts, local(): jnp.broadcast_to(target_embed[None], (sources,) + target_embed.shape)  2.64 us
  transfers between devices with their start and end apart: 11, of which 9 were waited for; matrix products, arithmetic and copies ran while one was open for 0% of the time, Pallas kernels for 0%

profile of v1, /device:TPU:0, one launch (start us, length us, event | category | flops | bytes accessed | tf_op | source)
XLA Modules:
  0.0 111.0 jit_solution(707619725552587473)
XLA Ops:
  0.6 2.6 %broadcast_in_dim.4 = bf16[16,2,16384]{2,1,0:T(2,128)(2,1)} broadcast(bf16[2,16384]{1,0:T(2,128)(2,1)} %param.8), dimensions={1,2} | broadcast | bytes 1114112 | tf_op jit(solution)/shard_map/broadcast_in_dim | solution.py:125
  3.3 0.0 copy-start.3
  3.3 8.1 %all-to-all-start = ((bf16[16,2,16384]{2,1,0:T(2,128)(2,1)}), bf16[16,2,16384]{2,1,0:T(2,128)(2,1)S(1)}, u32[]{:S(2)}, u32[]{:S(2)}) async-start(bf16[16,2,16384]{2,1,0:T(2,128)(2,1)} %broadcast_in_dim.4), calls=%async_computation | async-start | bytes 2097152 | tf_op jit(solution)/shard_map/all_to_all | solution.py:126
  11.4 0.0 copy-done.3
  11.4 13.6 %all-gather = bf16[8,4,8192]{2,1,0:T(4,128)(2,1)S(1)} all-gather(bf16[1,4,8192]{2,1,0:T(4,128)(2,1)S(1)} %bitcast.13), channel_id=1, replica_groups=mesh['src'=16,'tgt'=8] {'tgt'}, dimensions={0}, use_global_device_ids=true | all-gather | bytes 589824 | tf_op jit(solution)/shard_map/all_gather | solution.py:127
  25.0 0.1 reshape.12.keep_ref.red_ref
  25.8 0.0 copy-start.1
  25.8 3.3 %all-to-all-done = bf16[16,2,16384]{2,1,0:T(2,128)(2,1)S(1)} async-done(((bf16[16,2,16384]{2,1,0:T(2,128)(2,1)}), bf16[16,2,16384]{2,1,0:T(2,128)(2,1)S(1)}, u32[]{:S(2)}, u32[]{:S(2)}) %all-to-all-start) | async-done | bytes 1048608 | tf_op jit(solution)/shard_map/all_to_all | solution.py:126
  29.1 0.4 reshape.10.red_ref.keep_ref
  29.5 0.0 copy-start.2
  29.5 0.0 copy-done.1
  29.5 0.7 copy-done.2
  30.2 8.7 %row_lse.1 = f32[1,8192]{1,0:T(1,128)S(1)} custom-call(s32[2,64]{1,0:T(2,128)S(1)} %bitcast.9, s32[1,1]{1,0:T(1,128)S(6)} %copy.9.count_ref, bf16[32,16384]{1,0:T(8,128)(2,1)S(1)} %reshape.10.red_ref.keep_ref, bf16[32,8192]{1,0:T(8,128)(2,1)S(1)} %reshape.12.keep_ref.red_ref, f32[1,16384]{1,0:T(1,128)S(1)} %bitcast.8), custom_call_target="tpu_custom_call" | custom-call | tf_op jit(solution)/shard_map/row_lse/pallas_call | solution.py:93
  38.8 0.0 copy-start.5
  38.9 0.1 collective-permute-start
  38.9 1.2 %collective-permute-done = f32[1,8192]{1,0:T(1,128)S(1)} collective-permute-done((f32[1,8192]{1,0:T(1,128)S(1)}, f32[1,8192]{1,0:T(1,128)S(1)}, u32[]{:S(2)}, u32[]{:S(2)}) %collective-permute-start) | collective-permute-done | bytes 32800 | tf_op jit(solution)/shard_map/ppermute | solution.py:120
  40.1 0.1 multiply_add_fusion.1
  40.3 3.5 %collective-permute-start.1 = (f32[1,8192]{1,0:T(1,128)S(1)}, f32[1,8192]{1,0:T(1,128)S(1)}, u32[]{:S(2)}, u32[]{:S(2)}) collective-permute-start(f32[1,8192]{1,0:T(1,128)S(1)} %multiply_add_fusion.1), channel_id=1, source_target_pairs={{0,2},{1,3},{2,4},{3,5},{4,6},{5,7},{6,0},{7,1},{8,10},{9,11},{10,... | collective-permute-start | bytes 98312 | tf_op jit(solution)/shard_map/ppermute | solution.py:120
  43.7 11.2 %collective-permute-start.2 = (f32[1,8192]{1,0:T(1,128)S(1)}, f32[1,8192]{1,0:T(1,128)S(1)}, u32[]{:S(2)}, u32[]{:S(2)}) collective-permute-start(f32[1,8192]{1,0:T(1,128)S(1)} %multiply_add_fusion.1), channel_id=1, source_target_pairs={{0,4},{1,5},{2,6},{3,7},{4,0},{5,1},{6,2},{7,3},{8,12},{9,13},{10,... | collective-permute-start | bytes 98312 | tf_op jit(solution)/shard_map/ppermute | solution.py:120
  55.0 0.0 collective-permute-start.3
  55.0 0.0 copy-done.5
  55.0 0.4 collective-permute-done.1
  55.4 1.8 %collective-permute-done.2 = f32[1,8192]{1,0:T(1,128)S(1)} collective-permute-done((f32[1,8192]{1,0:T(1,128)S(1)}, f32[1,8192]{1,0:T(1,128)S(1)}, u32[]{:S(2)}, u32[]{:S(2)}) %collective-permute-start.2) | collective-permute-done | bytes 32800 | tf_op jit(solution)/shard_map/ppermute | solution.py:120
  57.2 1.7 %collective-permute-done.3 = f32[1,8192]{1,0:T(1,128)S(1)} collective-permute-done((f32[1,8192]{1,0:T(1,128)S(1)}, f32[1,8192]{1,0:T(1,128)S(1)}, u32[]{:S(2)}, u32[]{:S(2)}) %collective-permute-start.3) | collective-permute-done | bytes 32800 | tf_op jit(solution)/shard_map/ppermute | solution.py:120
  58.9 0.3 multiply_subtract_fusion.1.bias_ref
  59.1 0.0 copy-start
  59.1 7.3 %column_lse.1 = f32[1,16384]{1,0:T(1,128)S(1)} custom-call(s32[2,64]{1,0:T(2,128)S(1)} %bitcast.10, s32[1,1]{1,0:T(1,128)S(6)} %copy.9.count_ref, bf16[32,8192]{1,0:T(8,128)(2,1)S(1)} %reshape.12.keep_ref.red_ref, bf16[32,16384]{1,0:T(8,128)(2,1)S(1)} %reshape.10.red_ref.keep_ref, f32[1,8192]{1,0:T(1,128)S(1)} %multiply_subtract_fusion.1.bias_ref), custom_call_target="tpu_custom_call" | custom-call | tf_op jit(solution)/shard_map/column_lse/pallas_call | solution.py:93
  66.5 0.0 copy-done
  66.5 0.0 copy-start.4
  66.5 0.6 collective-permute-start.4
  67.0 16.1 %collective-permute-start.5 = (f32[1,16384]{1,0:T(1,128)S(1)}, f32[1,16384]{1,0:T(1,128)S(1)}, u32[]{:S(2)}, u32[]{:S(2)}) collective-permute-start(f32[1,16384]{1,0:T(1,128)S(1)} %column_lse.1), channel_id=1, source_target_pairs={{0,64},{8,72},{16,80},{24,88},{32,96},{40,104},{48,112},{56,120},{... | collective-permute-start | bytes 196616 | tf_op jit(solution)/shard_map/ppermute | solution.py:120
  83.2 2.5 %collective-permute-start.6 = (f32[1,16384]{1,0:T(1,128)S(1)}, f32[1,16384]{1,0:T(1,128)S(1)}, u32[]{:S(2)}, u32[]{:S(2)}) collective-permute-start(f32[1,16384]{1,0:T(1,128)S(1)} %column_lse.1), channel_id=1, source_target_pairs={{0,96},{8,104},{16,112},{24,120},{32,0},{40,8},{48,16},{56,24},{64... | collective-permute-start | bytes 196616 | tf_op jit(solution)/shard_map/ppermute | solution.py:120
  85.7 0.0 collective-permute-done.4
  85.7 0.3 collective-permute-done.5
  86.0 1.6 %collective-permute-done.6 = f32[1,16384]{1,0:T(1,128)S(1)} collective-permute-done((f32[1,16384]{1,0:T(1,128)S(1)}, f32[1,16384]{1,0:T(1,128)S(1)}, u32[]{:S(2)}, u32[]{:S(2)}) %collective-permute-start.6) | collective-permute-done | bytes 65568 | tf_op jit(solution)/shard_map/ppermute | solution.py:120
  87.6 0.5 multiply_add_fusion
  88.1 13.9 %collective-permute-start.7 = (f32[1,16384]{1,0:T(1,128)S(1)}, f32[1,16384]{1,0:T(1,128)S(1)}, u32[]{:S(2)}, u32[]{:S(2)}) collective-permute-start(f32[1,16384]{1,0:T(1,128)S(1)} %multiply_add_fusion), channel_id=1, source_target_pairs={{0,8},{8,16},{16,24},{24,0},{32,40},{40,48},{48,56},{56,32},{64,72... | collective-permute-start | bytes 196616 | tf_op jit(solution)/shard_map/ppermute | solution.py:120
  102.0 3.6 %collective-permute-start.8 = (f32[1,16384]{1,0:T(1,128)S(1)}, f32[1,16384]{1,0:T(1,128)S(1)}, u32[]{:S(2)}, u32[]{:S(2)}) collective-permute-start(f32[1,16384]{1,0:T(1,128)S(1)} %multiply_add_fusion), channel_id=1, source_target_pairs={{0,16},{8,24},{16,0},{24,8},{32,48},{40,56},{48,32},{56,40},{64,80... | collective-permute-start | bytes 196616 | tf_op jit(solution)/shard_map/ppermute | solution.py:120
  105.6 1.0 collective-permute-start.9
  106.6 0.0 copy-done.4
  106.7 0.0 collective-permute-done.7
  106.7 1.9 %collective-permute-done.8 = f32[1,16384]{1,0:T(1,128)S(1)} collective-permute-done((f32[1,16384]{1,0:T(1,128)S(1)}, f32[1,16384]{1,0:T(1,128)S(1)}, u32[]{:S(2)}, u32[]{:S(2)}) %collective-permute-start.8) | collective-permute-done | bytes 65568 | tf_op jit(solution)/shard_map/ppermute | solution.py:120
  108.6 1.3 %collective-permute-done.9 = f32[1,16384]{1,0:T(1,128)S(1)} collective-permute-done((f32[1,16384]{1,0:T(1,128)S(1)}, f32[1,16384]{1,0:T(1,128)S(1)}, u32[]{:S(2)}, u32[]{:S(2)}) %collective-permute-start.9) | collective-permute-done | bytes 65568 | tf_op jit(solution)/shard_map/ppermute | solution.py:120
  109.9 1.1 %multiply_subtract_fusion = f32[1,16384]{1,0:T(1,128)} fusion(f32[1,16384]{1,0:T(1,128)S(1)} %bitcast.11, f32[1,16384]{1,0:T(1,128)S(1)} %collective-permute-done.9, f32[1,16384]{1,0:T(1,128)S(1)} %collective-permute-done.8, f32[1,16384]{1,0:T(1,128)S(1)} %collective-permute-done.7, f32[1,16384]{1,0:T(1,128)S(1)} %multiply_add_fusion), kind=kLoop, calls=%fused_computation | loop fusion | flops 294912 | bytes 393216 | tf_op jit(solution)/shard_map/sub | solution.py:138
  (2 shorter events, 0.0 us)
Async XLA Ops:
  3.3 8.1 %copy-start.3 = (bf16[4,8192]{1,0:T(4,128)(2,1)S(1)}, bf16[4,8192]{1,0:T(4,128)(2,1)}, u32[]{:S(2)}) copy-start(bf16[4,8192]{1,0:T(4,128)(2,1)} %param.7) | copy-start | bytes 196612
  3.3 25.8 %all-to-all-start = ((bf16[16,2,16384]{2,1,0:T(2,128)(2,1)}), bf16[16,2,16384]{2,1,0:T(2,128)(2,1)S(1)}, u32[]{:S(2)}, u32[]{:S(2)}) async-start(bf16[16,2,16384]{2,1,0:T(2,128)(2,1)} %broadcast_in_dim.4), calls=%async_computation | async-start | bytes 2097152 | tf_op jit(solution)/shard_map/all_to_all | solution.py:126
  25.8 3.7 %copy-start.1 = (f32[16384]{0:T(1024)S(1)}, f32[16384]{0:T(1024)}, u32[]{:S(2)}) copy-start(f32[16384]{0:T(1024)} %param.9) | copy-start | bytes 196612
  29.5 0.7 copy-start.2
  38.8 16.1 %copy-start.5 = (f32[8192]{0:T(1024)S(1)}, f32[8192]{0:T(1024)}, u32[]{:S(2)}) copy-start(f32[8192]{0:T(1024)} %param.10) | copy-start | bytes 98308
  38.9 1.3 %collective-permute-start = (f32[1,8192]{1,0:T(1,128)S(1)}, f32[1,8192]{1,0:T(1,128)S(1)}, u32[]{:S(2)}, u32[]{:S(2)}) collective-permute-start(f32[1,8192]{1,0:T(1,128)S(1)} %row_lse.1), channel_id=1, source_target_pairs={{0,1},{1,0},{2,3},{3,2},{4,5},{5,4},{6,7},{7,6},{8,9},{9,8},{10,11... | collective-permute-start | bytes 98312 | tf_op jit(solution)/shard_map/ppermute | solution.py:120
  40.3 15.1 %collective-permute-start.1 = (f32[1,8192]{1,0:T(1,128)S(1)}, f32[1,8192]{1,0:T(1,128)S(1)}, u32[]{:S(2)}, u32[]{:S(2)}) collective-permute-start(f32[1,8192]{1,0:T(1,128)S(1)} %multiply_add_fusion.1), channel_id=1, source_target_pairs={{0,2},{1,3},{2,4},{3,5},{4,6},{5,7},{6,0},{7,1},{8,10},{9,11},{10,... | collective-permute-start | bytes 98312 | tf_op jit(solution)/shard_map/ppermute | solution.py:120
  43.7 13.4 %collective-permute-start.2 = (f32[1,8192]{1,0:T(1,128)S(1)}, f32[1,8192]{1,0:T(1,128)S(1)}, u32[]{:S(2)}, u32[]{:S(2)}) collective-permute-start(f32[1,8192]{1,0:T(1,128)S(1)} %multiply_add_fusion.1), channel_id=1, source_target_pairs={{0,4},{1,5},{2,6},{3,7},{4,0},{5,1},{6,2},{7,3},{8,12},{9,13},{10,... | collective-permute-start | bytes 98312 | tf_op jit(solution)/shard_map/ppermute | solution.py:120
  55.0 3.9 %collective-permute-start.3 = (f32[1,8192]{1,0:T(1,128)S(1)}, f32[1,8192]{1,0:T(1,128)S(1)}, u32[]{:S(2)}, u32[]{:S(2)}) collective-permute-start(f32[1,8192]{1,0:T(1,128)S(1)} %multiply_add_fusion.1), channel_id=1, source_target_pairs={{0,6},{1,7},{2,0},{3,1},{4,2},{5,3},{6,4},{7,5},{8,14},{9,15},{10,... | collective-permute-start | bytes 98312 | tf_op jit(solution)/shard_map/ppermute | solution.py:120
  59.1 7.3 %copy-start = (f32[1,8192]{1,0:T(1,128)}, f32[1,8192]{1,0:T(1,128)S(1)}, u32[]{:S(2)}) copy-start(f32[1,8192]{1,0:T(1,128)S(1)} %multiply_subtract_fusion.1.bias_ref) | copy-start | bytes 98308
  66.5 40.2 %copy-start.4 = (f32[16384]{0:T(1024)S(1)}, f32[16384]{0:T(1024)}, u32[]{:S(2)}) copy-start(f32[16384]{0:T(1024)} %param.11) | copy-start | bytes 196612
  66.5 19.2 %collective-permute-start.4 = (f32[1,16384]{1,0:T(1,128)S(1)}, f32[1,16384]{1,0:T(1,128)S(1)}, u32[]{:S(2)}, u32[]{:S(2)}) collective-permute-start(f32[1,16384]{1,0:T(1,128)S(1)} %column_lse.1), channel_id=1, source_target_pairs={{0,32},{8,40},{16,48},{24,56},{32,64},{40,72},{48,80},{56,88},{64,... | collective-permute-start | bytes 196616 | tf_op jit(solution)/shard_map/ppermute | solution.py:120
  67.0 19.0 %collective-permute-start.5 = (f32[1,16384]{1,0:T(1,128)S(1)}, f32[1,16384]{1,0:T(1,128)S(1)}, u32[]{:S(2)}, u32[]{:S(2)}) collective-permute-start(f32[1,16384]{1,0:T(1,128)S(1)} %column_lse.1), channel_id=1, source_target_pairs={{0,64},{8,72},{16,80},{24,88},{32,96},{40,104},{48,112},{56,120},{... | collective-permute-start | bytes 196616 | tf_op jit(solution)/shard_map/ppermute | solution.py:120
  83.2 4.4 %collective-permute-start.6 = (f32[1,16384]{1,0:T(1,128)S(1)}, f32[1,16384]{1,0:T(1,128)S(1)}, u32[]{:S(2)}, u32[]{:S(2)}) collective-permute-start(f32[1,16384]{1,0:T(1,128)S(1)} %column_lse.1), channel_id=1, source_target_pairs={{0,96},{8,104},{16,112},{24,120},{32,0},{40,8},{48,16},{56,24},{64... | collective-permute-start | bytes 196616 | tf_op jit(solution)/shard_map/ppermute | solution.py:120
  88.1 18.6 %collective-permute-start.7 = (f32[1,16384]{1,0:T(1,128)S(1)}, f32[1,16384]{1,0:T(1,128)S(1)}, u32[]{:S(2)}, u32[]{:S(2)}) collective-permute-start(f32[1,16384]{1,0:T(1,128)S(1)} %multiply_add_fusion), channel_id=1, source_target_pairs={{0,8},{8,16},{16,24},{24,0},{32,40},{40,48},{48,56},{56,32},{64,72... | collective-permute-start | bytes 196616 | tf_op jit(solution)/shard_map/ppermute | solution.py:120
  102.0 6.6 %collective-permute-start.8 = (f32[1,16384]{1,0:T(1,128)S(1)}, f32[1,16384]{1,0:T(1,128)S(1)}, u32[]{:S(2)}, u32[]{:S(2)}) collective-permute-start(f32[1,16384]{1,0:T(1,128)S(1)} %multiply_add_fusion), channel_id=1, source_target_pairs={{0,16},{8,24},{16,0},{24,8},{32,48},{40,56},{48,32},{56,40},{64,80... | collective-permute-start | bytes 196616 | tf_op jit(solution)/shard_map/ppermute | solution.py:120
  105.6 4.3 %collective-permute-start.9 = (f32[1,16384]{1,0:T(1,128)S(1)}, f32[1,16384]{1,0:T(1,128)S(1)}, u32[]{:S(2)}, u32[]{:S(2)}) collective-permute-start(f32[1,16384]{1,0:T(1,128)S(1)} %multiply_add_fusion), channel_id=1, source_target_pairs={{0,24},{8,0},{16,8},{24,16},{32,56},{40,32},{48,40},{56,48},{64,88... | collective-permute-start | bytes 196616 | tf_op jit(solution)/shard_map/ppermute | solution.py:120

commit v2 on v1

--- a/solution.py
+++ b/solution.py
@@ -52,7 +52,7 @@
     lax.fori_loop(0, red_tiles, prepare_reduced, 0)
     lax.fori_loop(0, keep_tiles, prepare_kept, 0)
 
-    lanes_of, rows_of = 256, 128
+    lanes_of, rows_of, together = 512, 64, 4
 
     def step(entry, _):
         red_at = pl.multiple_of(list_ref[red_row, entry] * TILE, TILE)
@@ -72,7 +72,15 @@
             total[:, lanes] = summed
         return 0
 
-    lax.fori_loop(0, count_ref[0, 0], step, 0)
+    def steps(group, _):
+        for member in range(together):
+            step(group * together + member, 0)
+        return 0
+
+    live = count_ref[0, 0]
+    whole = live // together
+    lax.fori_loop(0, whole, steps, 0)
+    lax.fori_loop(whole * together, live, step, 0)
 
     def finish(tile, _):
         at = at_tile(tile)

time: 111 us -> 95.2 us (0.86)
  the two profiles are of different devices: /device:TPU:0 before, /device:TPU:8 now
where the time goes in v2:
time: 95.2 us; the launch traced here: 93.8 us
  Pallas kernels  29.9 us (31%)
  starting transfers between devices  29.6 us (31%)
  waiting for transfers between devices  13.7 us (14%)
  blocking collectives  13.3 us (14%)
  local copies, waits for them, and re-layouts  3.86 us (4%)
  other arithmetic  1.98 us (2%)
  between operations  1.42 us (1%)
    pallas_call x2, Pallas kernels, block_lse(): pl.pallas_call(functools.partial(lse_kernel, red_row, 1 - red_row), name=...  29.9 us
    ppermute x10, starting transfers between devices, along(): return lambda value: lax.ppermute(value, axis, pairs)  21.6 us
    all_gather x1, blocking collectives, local(): source_full = lax.all_gather(source_embed, 'tgt', axis=0, tiled=True)  13.3 us
    ppermute x10, waiting for transfers between devices, along(): return lambda value: lax.ppermute(value, axis, pairs)  10.1 us
    all_to_all x1, starting transfers between devices, local(): target_full = lax.all_to_all(copies, 'src', 0, 0).reshape(WIDTH, -1)  8.01 us
    all_to_all x1, waiting for transfers between devices, local(): target_full = lax.all_to_all(copies, 'src', 0, 0).reshape(WIDTH, -1)  3.56 us
    broadcast_in_dim x1, local copies, waits for them, and re-layouts, local(): jnp.broadcast_to(target_embed[None], (sources,) + target_embed.shape)  2.64 us
  transfers between devices with their start and end apart: 11, of which 8 were waited for; matrix products, arithmetic and copies ran while one was open for 0% of the time, Pallas kernels for 0%

profile of v2, /device:TPU:8, one launch (start us, length us, event | category | flops | bytes accessed | tf_op | source)
XLA Modules:
  0.0 93.8 jit_solution(6696270071115475138)
XLA Ops:
  0.6 2.6 %broadcast_in_dim.4 = bf16[16,2,16384]{2,1,0:T(2,128)(2,1)} broadcast(bf16[2,16384]{1,0:T(2,128)(2,1)} %param.8), dimensions={1,2} | broadcast | bytes 1114112 | tf_op jit(solution)/shard_map/broadcast_in_dim | solution.py:133
  3.3 0.0 copy-start.3
  3.3 8.0 %all-to-all-start = ((bf16[16,2,16384]{2,1,0:T(2,128)(2,1)}), bf16[16,2,16384]{2,1,0:T(2,128)(2,1)S(1)}, u32[]{:S(2)}, u32[]{:S(2)}) async-start(bf16[16,2,16384]{2,1,0:T(2,128)(2,1)} %broadcast_in_dim.4), calls=%async_computation | async-start | bytes 2097152 | tf_op jit(solution)/shard_map/all_to_all | solution.py:134
  11.3 0.0 copy-done.3
  11.3 13.3 %all-gather = bf16[8,4,8192]{2,1,0:T(4,128)(2,1)S(1)} all-gather(bf16[1,4,8192]{2,1,0:T(4,128)(2,1)S(1)} %bitcast.13), channel_id=1, replica_groups=mesh['src'=16,'tgt'=8] {'tgt'}, dimensions={0}, use_global_device_ids=true | all-gather | bytes 589824 | tf_op jit(solution)/shard_map/all_gather | solution.py:135
  24.6 0.1 reshape.12.keep_ref.red_ref
  25.4 0.0 copy-start.1
  25.4 3.6 %all-to-all-done = bf16[16,2,16384]{2,1,0:T(2,128)(2,1)S(1)} async-done(((bf16[16,2,16384]{2,1,0:T(2,128)(2,1)}), bf16[16,2,16384]{2,1,0:T(2,128)(2,1)S(1)}, u32[]{:S(2)}, u32[]{:S(2)}) %all-to-all-start) | async-done | bytes 1048608 | tf_op jit(solution)/shard_map/all_to_all | solution.py:134
  29.0 0.4 reshape.10.red_ref.keep_ref
  29.4 0.0 copy-start.2
  29.4 0.0 copy-done.1
  29.4 0.7 copy-done.2
  30.1 15.6 %row_lse.1 = f32[1,8192]{1,0:T(1,128)S(1)} custom-call(s32[2,64]{1,0:T(2,128)S(1)} %bitcast.9, s32[1,1]{1,0:T(1,128)S(6)} %copy.9.count_ref, bf16[32,16384]{1,0:T(8,128)(2,1)S(1)} %reshape.10.red_ref.keep_ref, bf16[32,8192]{1,0:T(8,128)(2,1)S(1)} %reshape.12.keep_ref.red_ref, f32[1,16384]{1,0:T(1,128)S(1)} %bitcast.8), custom_call_target="tpu_custom_call" | custom-call | tf_op jit(solution)/shard_map/row_lse/pallas_call | solution.py:101
  45.7 0.0 copy-start.5
  45.8 0.1 collective-permute-start
  45.9 1.2 %collective-permute-done = f32[1,8192]{1,0:T(1,128)S(1)} collective-permute-done((f32[1,8192]{1,0:T(1,128)S(1)}, f32[1,8192]{1,0:T(1,128)S(1)}, u32[]{:S(2)}, u32[]{:S(2)}) %collective-permute-start) | collective-permute-done | bytes 32800 | tf_op jit(solution)/shard_map/ppermute | solution.py:128
  47.0 0.1 multiply_add_fusion.1
  47.2 2.6 %collective-permute-start.1 = (f32[1,8192]{1,0:T(1,128)S(1)}, f32[1,8192]{1,0:T(1,128)S(1)}, u32[]{:S(2)}, u32[]{:S(2)}) collective-permute-start(f32[1,8192]{1,0:T(1,128)S(1)} %multiply_add_fusion.1), channel_id=1, source_target_pairs={{0,2},{1,3},{2,4},{3,5},{4,6},{5,7},{6,0},{7,1},{8,10},{9,11},{10,... | collective-permute-start | bytes 98312 | tf_op jit(solution)/shard_map/ppermute | solution.py:128
  49.8 0.0 collective-permute-start.2
  49.8 2.2 %collective-permute-start.3 = (f32[1,8192]{1,0:T(1,128)S(1)}, f32[1,8192]{1,0:T(1,128)S(1)}, u32[]{:S(2)}, u32[]{:S(2)}) collective-permute-start(f32[1,8192]{1,0:T(1,128)S(1)} %multiply_add_fusion.1), channel_id=1, source_target_pairs={{0,6},{1,7},{2,0},{3,1},{4,2},{5,3},{6,4},{7,5},{8,14},{9,15},{10,... | collective-permute-start | bytes 98312 | tf_op jit(solution)/shard_map/ppermute | solution.py:128
  52.0 0.0 copy-done.5
  52.0 0.0 collective-permute-done.1
  52.0 3.2 %collective-permute-done.2 = f32[1,8192]{1,0:T(1,128)S(1)} collective-permute-done((f32[1,8192]{1,0:T(1,128)S(1)}, f32[1,8192]{1,0:T(1,128)S(1)}, u32[]{:S(2)}, u32[]{:S(2)}) %collective-permute-start.2) | collective-permute-done | bytes 32800 | tf_op jit(solution)/shard_map/ppermute | solution.py:128
  55.2 0.0 collective-permute-done.3
  55.2 0.3 multiply_subtract_fusion.1.bias_ref
  55.5 0.0 copy-start
  55.5 14.3 %column_lse.1 = f32[1,16384]{1,0:T(1,128)S(1)} custom-call(s32[2,64]{1,0:T(2,128)S(1)} %bitcast.10, s32[1,1]{1,0:T(1,128)S(6)} %copy.9.count_ref, bf16[32,8192]{1,0:T(8,128)(2,1)S(1)} %reshape.12.keep_ref.red_ref, bf16[32,16384]{1,0:T(8,128)(2,1)S(1)} %reshape.10.red_ref.keep_ref, f32[1,8192]{1,0:T(1,128)S(1)} %multiply_subtract_fusion.1.bias_ref), custom_call_target="tpu_custom_call" | custom-call | tf_op jit(solution)/shard_map/column_lse/pallas_call | solution.py:101
  69.8 0.0 copy-done
  69.8 0.0 copy-start.4
  69.8 2.5 %collective-permute-start.4 = (f32[1,16384]{1,0:T(1,128)S(1)}, f32[1,16384]{1,0:T(1,128)S(1)}, u32[]{:S(2)}, u32[]{:S(2)}) collective-permute-start(f32[1,16384]{1,0:T(1,128)S(1)} %column_lse.1), channel_id=1, source_target_pairs={{0,32},{8,40},{16,48},{24,56},{32,64},{40,72},{48,80},{56,88},{64,... | collective-permute-start | bytes 196616 | tf_op jit(solution)/shard_map/ppermute | solution.py:128
  72.3 2.3 %collective-permute-start.5 = (f32[1,16384]{1,0:T(1,128)S(1)}, f32[1,16384]{1,0:T(1,128)S(1)}, u32[]{:S(2)}, u32[]{:S(2)}) collective-permute-start(f32[1,16384]{1,0:T(1,128)S(1)} %column_lse.1), channel_id=1, source_target_pairs={{0,64},{8,72},{16,80},{24,88},{32,96},{40,104},{48,112},{56,120},{... | collective-permute-start | bytes 196616 | tf_op jit(solution)/shard_map/ppermute | solution.py:128
  74.6 0.5 collective-permute-start.6
  75.1 0.3 collective-permute-done.4
  75.4 2.7 %collective-permute-done.5 = f32[1,16384]{1,0:T(1,128)S(1)} collective-permute-done((f32[1,16384]{1,0:T(1,128)S(1)}, f32[1,16384]{1,0:T(1,128)S(1)}, u32[]{:S(2)}, u32[]{:S(2)}) %collective-permute-start.5) | collective-permute-done | bytes 65568 | tf_op jit(solution)/shard_map/ppermute | solution.py:128
  78.1 0.8 collective-permute-done.6
  78.9 0.5 multiply_add_fusion
  79.3 0.1 collective-permute-start.7
  79.4 8.9 %collective-permute-start.8 = (f32[1,16384]{1,0:T(1,128)S(1)}, f32[1,16384]{1,0:T(1,128)S(1)}, u32[]{:S(2)}, u32[]{:S(2)}) collective-permute-start(f32[1,16384]{1,0:T(1,128)S(1)} %multiply_add_fusion), channel_id=1, source_target_pairs={{0,16},{8,24},{16,0},{24,8},{32,48},{40,56},{48,32},{56,40},{64,80... | collective-permute-start | bytes 196616 | tf_op jit(solution)/shard_map/ppermute | solution.py:128
  88.3 2.5 %collective-permute-start.9 = (f32[1,16384]{1,0:T(1,128)S(1)}, f32[1,16384]{1,0:T(1,128)S(1)}, u32[]{:S(2)}, u32[]{:S(2)}) collective-permute-start(f32[1,16384]{1,0:T(1,128)S(1)} %multiply_add_fusion), channel_id=1, source_target_pairs={{0,24},{8,0},{16,8},{24,16},{32,56},{40,32},{48,40},{56,48},{64,88... | collective-permute-start | bytes 196616 | tf_op jit(solution)/shard_map/ppermute | solution.py:128
  90.8 0.0 copy-done.4
  90.8 0.0 collective-permute-done.7
  90.8 0.3 collective-permute-done.8
  91.1 1.6 %collective-permute-done.9 = f32[1,16384]{1,0:T(1,128)S(1)} collective-permute-done((f32[1,16384]{1,0:T(1,128)S(1)}, f32[1,16384]{1,0:T(1,128)S(1)}, u32[]{:S(2)}, u32[]{:S(2)}) %collective-permute-start.9) | collective-permute-done | bytes 65568 | tf_op jit(solution)/shard_map/ppermute | solution.py:128
  92.7 1.1 %multiply_subtract_fusion = f32[1,16384]{1,0:T(1,128)} fusion(f32[1,16384]{1,0:T(1,128)S(1)} %bitcast.11, f32[1,16384]{1,0:T(1,128)S(1)} %collective-permute-done.9, f32[1,16384]{1,0:T(1,128)S(1)} %collective-permute-done.8, f32[1,16384]{1,0:T(1,128)S(1)} %collective-permute-done.7, f32[1,16384]{1,0:T(1,128)S(1)} %multiply_add_fusion), kind=kLoop, calls=%fused_computation | loop fusion | flops 294912 | bytes 393216 | tf_op jit(solution)/shard_map/sub | solution.py:146
  (2 shorter events, 0.0 us)
Async XLA Ops:
  3.3 8.0 %copy-start.3 = (bf16[4,8192]{1,0:T(4,128)(2,1)S(1)}, bf16[4,8192]{1,0:T(4,128)(2,1)}, u32[]{:S(2)}) copy-start(bf16[4,8192]{1,0:T(4,128)(2,1)} %param.7) | copy-start | bytes 196612
  3.3 25.7 %all-to-all-start = ((bf16[16,2,16384]{2,1,0:T(2,128)(2,1)}), bf16[16,2,16384]{2,1,0:T(2,128)(2,1)S(1)}, u32[]{:S(2)}, u32[]{:S(2)}) async-start(bf16[16,2,16384]{2,1,0:T(2,128)(2,1)} %broadcast_in_dim.4), calls=%async_computation | async-start | bytes 2097152 | tf_op jit(solution)/shard_map/all_to_all | solution.py:134
  25.4 4.0 %copy-start.1 = (f32[16384]{0:T(1024)S(1)}, f32[16384]{0:T(1024)}, u32[]{:S(2)}) copy-start(f32[16384]{0:T(1024)} %param.9) | copy-start | bytes 196612
  29.4 0.7 copy-start.2
  45.7 6.2 %copy-start.5 = (f32[8192]{0:T(1024)S(1)}, f32[8192]{0:T(1024)}, u32[]{:S(2)}) copy-start(f32[8192]{0:T(1024)} %param.10) | copy-start | bytes 98308
  45.8 1.3 %collective-permute-start = (f32[1,8192]{1,0:T(1,128)S(1)}, f32[1,8192]{1,0:T(1,128)S(1)}, u32[]{:S(2)}, u32[]{:S(2)}) collective-permute-start(f32[1,8192]{1,0:T(1,128)S(1)} %row_lse.1), channel_id=1, source_target_pairs={{0,1},{1,0},{2,3},{3,2},{4,5},{5,4},{6,7},{7,6},{8,9},{9,8},{10,11... | collective-permute-start | bytes 98312 | tf_op jit(solution)/shard_map/ppermute | solution.py:128
  47.2 4.8 %collective-permute-start.1 = (f32[1,8192]{1,0:T(1,128)S(1)}, f32[1,8192]{1,0:T(1,128)S(1)}, u32[]{:S(2)}, u32[]{:S(2)}) collective-permute-start(f32[1,8192]{1,0:T(1,128)S(1)} %multiply_add_fusion.1), channel_id=1, source_target_pairs={{0,2},{1,3},{2,4},{3,5},{4,6},{5,7},{6,0},{7,1},{8,10},{9,11},{10,... | collective-permute-start | bytes 98312 | tf_op jit(solution)/shard_map/ppermute | solution.py:128
  49.8 5.4 %collective-permute-start.2 = (f32[1,8192]{1,0:T(1,128)S(1)}, f32[1,8192]{1,0:T(1,128)S(1)}, u32[]{:S(2)}, u32[]{:S(2)}) collective-permute-start(f32[1,8192]{1,0:T(1,128)S(1)} %multiply_add_fusion.1), channel_id=1, source_target_pairs={{0,4},{1,5},{2,6},{3,7},{4,0},{5,1},{6,2},{7,3},{8,12},{9,13},{10,... | collective-permute-start | bytes 98312 | tf_op jit(solution)/shard_map/ppermute | solution.py:128
  49.8 5.4 %collective-permute-start.3 = (f32[1,8192]{1,0:T(1,128)S(1)}, f32[1,8192]{1,0:T(1,128)S(1)}, u32[]{:S(2)}, u32[]{:S(2)}) collective-permute-start(f32[1,8192]{1,0:T(1,128)S(1)} %multiply_add_fusion.1), channel_id=1, source_target_pairs={{0,6},{1,7},{2,0},{3,1},{4,2},{5,3},{6,4},{7,5},{8,14},{9,15},{10,... | collective-permute-start | bytes 98312 | tf_op jit(solution)/shard_map/ppermute | solution.py:128
  55.5 14.3 %copy-start = (f32[1,8192]{1,0:T(1,128)}, f32[1,8192]{1,0:T(1,128)S(1)}, u32[]{:S(2)}) copy-start(f32[1,8192]{1,0:T(1,128)S(1)} %multiply_subtract_fusion.1.bias_ref) | copy-start | bytes 98308
  69.8 21.0 %copy-start.4 = (f32[16384]{0:T(1024)S(1)}, f32[16384]{0:T(1024)}, u32[]{:S(2)}) copy-start(f32[16384]{0:T(1024)} %param.11) | copy-start | bytes 196612
  69.8 5.6 %collective-permute-start.4 = (f32[1,16384]{1,0:T(1,128)S(1)}, f32[1,16384]{1,0:T(1,128)S(1)}, u32[]{:S(2)}, u32[]{:S(2)}) collective-permute-start(f32[1,16384]{1,0:T(1,128)S(1)} %column_lse.1), channel_id=1, source_target_pairs={{0,32},{8,40},{16,48},{24,56},{32,64},{40,72},{48,80},{56,88},{64,... | collective-permute-start | bytes 196616 | tf_op jit(solution)/shard_map/ppermute | solution.py:128
  72.3 5.8 %collective-permute-start.5 = (f32[1,16384]{1,0:T(1,128)S(1)}, f32[1,16384]{1,0:T(1,128)S(1)}, u32[]{:S(2)}, u32[]{:S(2)}) collective-permute-start(f32[1,16384]{1,0:T(1,128)S(1)} %column_lse.1), channel_id=1, source_target_pairs={{0,64},{8,72},{16,80},{24,88},{32,96},{40,104},{48,112},{56,120},{... | collective-permute-start | bytes 196616 | tf_op jit(solution)/shard_map/ppermute | solution.py:128
  74.6 4.3 %collective-permute-start.6 = (f32[1,16384]{1,0:T(1,128)S(1)}, f32[1,16384]{1,0:T(1,128)S(1)}, u32[]{:S(2)}, u32[]{:S(2)}) collective-permute-start(f32[1,16384]{1,0:T(1,128)S(1)} %column_lse.1), channel_id=1, source_target_pairs={{0,96},{8,104},{16,112},{24,120},{32,0},{40,8},{48,16},{56,24},{64... | collective-permute-start | bytes 196616 | tf_op jit(solution)/shard_map/ppermute | solution.py:128
  79.3 11.5 %collective-permute-start.7 = (f32[1,16384]{1,0:T(1,128)S(1)}, f32[1,16384]{1,0:T(1,128)S(1)}, u32[]{:S(2)}, u32[]{:S(2)}) collective-permute-start(f32[1,16384]{1,0:T(1,128)S(1)} %multiply_add_fusion), channel_id=1, source_target_pairs={{0,8},{8,16},{16,24},{24,0},{32,40},{40,48},{48,56},{56,32},{64,72... | collective-permute-start | bytes 196616 | tf_op jit(solution)/shard_map/ppermute | solution.py:128
  79.4 11.7 %collective-permute-start.8 = (f32[1,16384]{1,0:T(1,128)S(1)}, f32[1,16384]{1,0:T(1,128)S(1)}, u32[]{:S(2)}, u32[]{:S(2)}) collective-permute-start(f32[1,16384]{1,0:T(1,128)S(1)} %multiply_add_fusion), channel_id=1, source_target_pairs={{0,16},{8,24},{16,0},{24,8},{32,48},{40,56},{48,32},{56,40},{64,80... | collective-permute-start | bytes 196616 | tf_op jit(solution)/shard_map/ppermute | solution.py:128
  88.3 4.4 %collective-permute-start.9 = (f32[1,16384]{1,0:T(1,128)S(1)}, f32[1,16384]{1,0:T(1,128)S(1)}, u32[]{:S(2)}, u32[]{:S(2)}) collective-permute-start(f32[1,16384]{1,0:T(1,128)S(1)} %multiply_add_fusion), channel_id=1, source_target_pairs={{0,24},{8,0},{16,8},{24,16},{32,56},{40,32},{48,40},{56,48},{64,88... | collective-permute-start | bytes 196616 | tf_op jit(solution)/shard_map/ppermute | solution.py:128

commit v3 on v1

v3 whole, which is shorter than its diff:
```python
import functools

import jax
import jax.numpy as jnp
from jax import lax
from jax.experimental import pallas as pl
from jax.experimental.pallas import tpu as pltpu
from jax.sharding import PartitionSpec as P

TILE = 512
WIDTH = 32
PIECES = 3
LEFT = 128
RIGHT = 112
DEPTH = 48
TOGETHER = 8
STORES = 4
EPSILON = 0.1
KAPPA = 1.4426950408889634 / EPSILON
ALPHA = KAPPA / WIDTH
GAMMA = KAPPA / (2 * WIDTH)
LOWEST = -1e30
TRUSTED = 2.0**-90

BF16, F32 = jnp.bfloat16, jnp.float32
VMEM = pl.BlockSpec(memory_space=pltpu.VMEM)
SMEM = pl.BlockSpec(memory_space=pltpu.SMEM)
ANY = pl.BlockSpec(memory_space=pl.ANY)


def at_tile(tile):
    return pl.ds(pl.multiple_of(tile * TILE, TILE), TILE)


def pieces(value, number=PIECES):
    terms = []
    for _ in range(number):
        terms.append(value.astype(BF16).astype(F32))
        value = value - terms[-1]
    return terms


def squares(cells):
    return jnp.sum(cells * cells, axis=0, keepdims=True)


def general_lse(red_row, keep_row, list_ref, live, red_ref, keep_ref, bias_ref, out_ref, top, total):
    keep_tiles = keep_ref.shape[1] // TILE
    half, scale = float(WIDTH), ALPHA
    rows_of = 64

    def clear(tile, _):
        at = at_tile(tile)
        top[:, at] = jnp.full((8, TILE), LOWEST, F32)
        total[:, at] = jnp.zeros((8, TILE), F32)
        return 0

    def step(entry, _):
        red_at = at_tile(list_ref[red_row, entry])
        keep_at = at_tile(list_ref[keep_row, entry])
        cells = red_ref[:, red_at].astype(F32)
        terms = pieces(half * bias_ref[:, red_at] - 0.5 * squares(cells))
        filler = jnp.zeros((DEPTH - WIDTH - PIECES, TILE), F32)
        left = jnp.transpose(jnp.concatenate([cells] + terms + [filler, jnp.zeros((LEFT - DEPTH, TILE), F32)], axis=0))
        left = left.astype(BF16)[:, :DEPTH]
        right = jnp.concatenate([keep_ref[:, keep_at].astype(F32), jnp.ones((PIECES, TILE), F32), filler], axis=0).astype(BF16)
        highest, summed = top[:, keep_at], total[:, keep_at]
        for row in range(0, TILE, rows_of):
            z = jnp.dot(left[row : row + rows_of], right, preferred_element_type=F32)
            z = z.reshape(rows_of // 8, 8, TILE) * scale
            higher = jnp.maximum(highest, jnp.max(z, axis=0))
            summed = summed * jnp.exp2(highest - higher) + jnp.sum(jnp.exp2(z - higher[None]), axis=0)
            highest = higher
        top[:, keep_at] = highest
        total[:, keep_at] = summed
        return 0

    def finish(tile, _):
        at = at_tile(tile)
        highest = jnp.max(top[:, at], axis=0, keepdims=True)
        summed = jnp.sum(total[:, at] * jnp.exp2(top[:, at] - highest), axis=0, keepdims=True)
        value = highest * (1.0 / KAPPA) + EPSILON * jnp.log(jnp.maximum(summed, 1.0))
        out_ref[:, at] = value - squares(keep_ref[:, at].astype(F32)) * (0.5 / WIDTH)
        return 0

    lax.fori_loop(0, keep_tiles, clear, 0)
    lax.fori_loop(0, live, step, 0)
    lax.fori_loop(0, keep_tiles, finish, 0)


def source_kernel(source_ref, left_ref):
    def prepare(tile, _):
        at = at_tile(tile)
        cells = source_ref[:, at].astype(F32)
        rows = pieces(cells * ALPHA) + [jnp.ones((PIECES, TILE), F32)] + pieces(squares(cells) * -GAMMA)
        rows.append(jnp.zeros((LEFT - PIECES * WIDTH - 2 * PIECES, TILE), F32))
        left_ref[at, :] = jnp.transpose(jnp.concatenate(rows, axis=0)).astype(BF16)
        return 0

    lax.fori_loop(0, source_ref.shape[1] // TILE, prepare, 0)


def groups(live, body):
    def one(group, _):
        for member in range(TOGETHER):
            entry = group * TOGETHER + member
            body(entry, member % STORES, entry // STORES)
        return 0

    lax.fori_loop(0, (live + TOGETHER - 1) // TOGETHER, one, 0)


def clear_marks(marks):
    for tile in range(marks.shape[0]):
        marks[tile] = 0


def row_kernel(
    list_ref, count_ref, left_ref, target_ref, potential_ref, source_hbm,
    out_ref, store_0, store_1, store_2, store_3,
    right, weight, sums, covered, smallest, top, total, source_ref, semaphore,
):
    stores = (store_0, store_1, store_2, store_3)
    source_tiles = left_ref.shape[0] // TILE
    target_tiles = target_ref.shape[1] // TILE
    live = count_ref[0, 0]
    highest = jnp.max(potential_ref[...], axis=1, keepdims=True)
    rows_of = 64

    def clear(tile, _):
        sums[at_tile(tile), :] = jnp.zeros((TILE, 128), F32)
        return 0

    def prepare(tile, _):
        at = at_tile(tile)
        cells = target_ref[:, at]
        for piece in range(PIECES):
            right[piece * WIDTH : (piece + 1) * WIDTH, at] = cells
        tail = pieces(squares(cells.astype(F32)) * -GAMMA) + [jnp.ones((PIECES, TILE), F32)]
        tail.append(jnp.zeros((RIGHT - PIECES * WIDTH - 2 * PIECES, TILE), F32))
        right[PIECES * WIDTH : RIGHT, at] = jnp.concatenate(tail, axis=0).astype(BF16)
        weight[:, at] = jnp.exp2((potential_ref[:, at] - highest) * KAPPA)
        return 0

    clear_marks(covered)
    lax.fori_loop(0, source_tiles, clear, 0)
    lax.fori_loop(0, target_tiles, prepare, 0)

    def step(entry, store, slot):
        alive = (entry < live).astype(jnp.int32)
        source_tile = list_ref[0, entry]
        target_at = at_tile(list_ref[1, entry])
        covered[source_tile] = jnp.maximum(covered[source_tile], alive)
        factor = weight[:, target_at] * alive.astype(F32)
        columns = right[:, target_at]
        for row in range(0, TILE, rows_of):
            at = pl.ds(pl.multiple_of(source_tile * TILE + row, rows_of), rows_of)
            value = jnp.exp2(jnp.dot(left_ref[at, :RIGHT], columns, preferred_element_type=F32))
            stores[store][slot, row : row + rows_of, :] = value.astype(BF16)
            value = value * factor
            sums[at, :] += (value[:, 0:128] + value[:, 128:256]) + (value[:, 256:384] + value[:, 384:512])

    groups(live, step)
    smallest[...] = jnp.ones((1, TILE), F32)

    def finish(tile, _):
        at = at_tile(tile)
        lines = sum(
            lax.dot_general(jnp.ones((16, 128), BF16), piece.astype(BF16), (((1,), (1,)), ((), ())), preferred_element_type=F32)
            for piece in pieces(sums[at, :], 2)
        )
        summed = lines[0:1]
        present = covered[tile] > 0
        value = highest + EPSILON * jnp.log(jnp.maximum(summed, TRUSTED))
        out_ref[:, at] = jnp.where(present, value, LOWEST)
        smallest[...] = jnp.minimum(smallest[...], jnp.where(present, summed, 1.0))
        return 0

    lax.fori_loop(0, source_tiles, finish, 0)

    @pl.when(jnp.min(smallest[...]) < TRUSTED)
    def _():
        copy = pltpu.make_async_copy(source_hbm, source_ref, semaphore)
        copy.start()
        copy.wait()
        general_lse(1, 0, list_ref, live, target_ref, source_ref, potential_ref, out_ref, top, total)


def column_kernel(
    list_ref, count_ref, potential_ref, store_0, store_1, store_2, store_3, source_hbm, target_hbm,
    out_ref,
    weight, sums, covered, smallest, top, total, source_ref, target_ref, semaphore,
):
    stores = (store_0, store_1, store_2, store_3)
    source_tiles = source_ref.shape[1] // TILE
    target_tiles = target_ref.shape[1] // TILE
    live = count_ref[0, 0]
    highest = jnp.max(potential_ref[...], axis=1, keepdims=True)

    def prepare(tile, _):
        at = at_tile(tile)
        terms = pieces(jnp.exp2((potential_ref[:, at] - highest) * KAPPA))
        weight[:, at] = jnp.concatenate(terms + [jnp.zeros((16 - PIECES, TILE), F32)], axis=0).astype(BF16)
        return 0

    def clear(tile, _):
        sums[:, at_tile(tile)] = jnp.zeros((16, TILE), F32)
        return 0

    clear_marks(covered)
    lax.fori_loop(0, source_tiles, prepare, 0)
    lax.fori_loop(0, target_tiles, clear, 0)

    def step(entry, store, slot):
        alive = (entry < live).astype(jnp.int32)
        target_tile = list_ref[1, entry]
        covered[target_tile] = jnp.maximum(covered[target_tile], alive)
        lines = jnp.dot(weight[:, at_tile(list_ref[0, entry])], stores[store][slot], preferred_element_type=F32)
        sums[:, at_tile(target_tile)] += lines * alive.astype(F32)

    groups(live, step)
    smallest[...] = jnp.ones((1, TILE), F32)

    def finish(tile, _):
        at = at_tile(tile)
        summed = jnp.sum(sums[:, at], axis=0, keepdims=True)
        present = covered[tile] > 0
        value = highest + EPSILON * jnp.log(jnp.maximum(summed, TRUSTED))
        out_ref[:, at] = jnp.where(present, value, LOWEST)
        smallest[...] = jnp.minimum(smallest[...], jnp.where(present, summed, 1.0))
        return 0

    lax.fori_loop(0, target_tiles, finish, 0)

    @pl.when(jnp.min(smallest[...]) < TRUSTED)
    def _():
        for hbm, ref in ((source_hbm, source_ref), (target_hbm, target_ref)):
            copy = pltpu.make_async_copy(hbm, ref, semaphore)
            copy.start()
            copy.wait()
        general_lse(0, 1, list_ref, live, source_ref, target_ref, potential_ref, out_ref, top, total)


def merged(parts):
    highest = functools.reduce(jnp.maximum, parts)
    summed = sum(jnp.exp((part - highest) * (1.0 / EPSILON)) for part in parts)
    return highest + EPSILON * jnp.log(summed)


def along(axis, size, group, stride, shift):
    pairs = []
    for index in range(size):
        digit = index // stride % group
        pairs.append((index, index + ((digit + shift) % group - digit) * stride))
    return lambda value: lax.ppermute(value, axis, pairs)


def local(source_embed, target_embed, target_potential, log_source_mass, log_target_mass, tile_list, counts):
    sources = lax.axis_size("src")
    copies = jnp.broadcast_to(target_embed[None], (sources,) + target_embed.shape)
    target_full = lax.all_to_all(copies, "src", 0, 0).reshape(WIDTH, -1)
    source_full = lax.all_gather(source_embed, "tgt", axis=0, tiled=True)
    own_list = tile_list[0, 0]
    source_cells, target_cells = source_full.shape[1], target_full.shape[1]
    slots = own_list.shape[1] // STORES

    left = pl.pallas_call(
        source_kernel,
        name="source_side",
        out_shape=pltpu.VMEM((source_cells, LEFT), BF16),
        in_specs=[VMEM],
        out_specs=VMEM,
        compiler_params=pltpu.CompilerParams(vmem_limit_bytes=10 << 20),
    )(source_full)

    row, *stores = pl.pallas_call(
        row_kernel,
        name="row_sums",
        out_shape=(jax.ShapeDtypeStruct((1, source_cells), F32),) + (pltpu.VMEM((slots, TILE, TILE), BF16),) * STORES,
        in_specs=[SMEM, SMEM, VMEM, VMEM, VMEM, ANY],
        out_specs=(VMEM,) * (1 + STORES),
        scratch_shapes=[
            pltpu.VMEM((RIGHT, target_cells), BF16),
            pltpu.VMEM((1, target_cells), F32),
            pltpu.VMEM((source_cells, 128), F32),
            pltpu.SMEM((source_cells // TILE,), jnp.int32),
            pltpu.VMEM((1, TILE), F32),
            pltpu.VMEM((8, source_cells), F32),
            pltpu.VMEM((8, source_cells), F32),
            pltpu.VMEM((WIDTH, source_cells), BF16),
            pltpu.SemaphoreType.DMA,
        ],
        compiler_params=pltpu.CompilerParams(vmem_limit_bytes=12 << 20),
    )(own_list, counts, left, target_full, target_potential[None], source_full)

    row = merged([row, along("tgt", 8, 2, 1, 1)(row)])
    row = merged([row] + [along("tgt", 8, 4, 2, shift)(row) for shift in (1, 2, 3)])
    row_potential = EPSILON * log_source_mass[None] - row

    column = pl.pallas_call(
        column_kernel,
        name="column_sums",
        out_shape=jax.ShapeDtypeStruct((1, target_cells), F32),
        in_specs=[SMEM, SMEM, VMEM] + [VMEM] * STORES + [ANY, ANY],
        out_specs=VMEM,
        scratch_shapes=[
            pltpu.VMEM((16, source_cells), BF16),
            pltpu.VMEM((16, target_cells), F32),
            pltpu.SMEM((target_cells // TILE,), jnp.int32),
            pltpu.VMEM((1, TILE), F32),
            pltpu.VMEM((8, target_cells), F32),
            pltpu.VMEM((8, target_cells), F32),
            pltpu.VMEM((WIDTH, source_cells), BF16),
            pltpu.VMEM((WIDTH, target_cells), BF16),
            pltpu.SemaphoreType.DMA,
        ],
        compiler_params=pltpu.CompilerParams(vmem_limit_bytes=10 << 20),
    )(own_list, counts, row_potential, *stores, source_full, target_full)

    column = merged([column] + [along("src", 16, 4, 4, shift)(column) for shift in (1, 2, 3)])
    column = merged([column] + [along("src", 16, 4, 1, shift)(column) for shift in (1, 2, 3)])
    column_potential = EPSILON * log_target_mass[None] - column
    return row_potential[0], column_potential[0]


def solution(mesh):
    return jax.shard_map(
        local,
        mesh=mesh,
        in_specs=(
            P("tgt", "src"),
            P("src", "tgt"),
            P("tgt"),
            P("src"),
            P("tgt"),
            P("src", "tgt", None, None),
            P("src", "tgt"),
        ),
        out_specs=(P("src"), P("tgt")),
        check_vma=False,
    )
```

time: 111 us -> 144 us (1.30)
  the two profiles are of different devices: /device:TPU:0 before, /device:TPU:24 now
where the time goes in v3:
time: 144 us; the launch traced here: 142 us
  starting transfers between devices  84.4 us (59%)
  Pallas kernels  21.7 us (15%)
  blocking collectives  13.3 us (9%)
  waiting for transfers between devices  13.1 us (9%)
  local copies, waits for them, and re-layouts  6.13 us (4%)
  other arithmetic  1.95 us (1%)
  between operations  1.44 us (1%)
    ppermute x10, starting transfers between devices, along(): return lambda value: lax.ppermute(value, axis, pairs)  76.5 us
    all_gather x1, blocking collectives, local(): source_full = lax.all_gather(source_embed, 'tgt', axis=0, tiled=True)  13.3 us
    ppermute x10, waiting for transfers between devices, along(): return lambda value: lax.ppermute(value, axis, pairs)  12.6 us
    pallas_call x1, Pallas kernels, local(): pl.pallas_call(row_kernel, name='row_sums', out_shape=(jax.ShapeDtypeStru...  11.2 us
    pallas_call x1, Pallas kernels, local(): pl.pallas_call(column_kernel, name='column_sums', out_shape=jax.ShapeDtyp...  8.6 us
    all_to_all x1, starting transfers between devices, local(): target_full = lax.all_to_all(copies, 'src', 0, 0).reshape(WIDTH, -1)  7.88 us
    unnamed x15, local copies, waits for them, and re-layouts  3.06 us
  transfers between devices with their start and end apart: 11, of which 8 were waited for; matrix products, arithmetic and copies ran while one was open for 0% of the time, Pallas kernels for 1%

profile of v3, /device:TPU:24, one launch (start us, length us, event | category | flops | bytes accessed | tf_op | source)
XLA Modules:
  0.0 141.9 jit_solution(6282695879309289817)
XLA Ops:
  0.6 0.0 copy-start.4
  0.6 0.0 copy-start.3
  0.7 0.0 copy-start.6
  0.7 2.6 %broadcast_in_dim.4 = bf16[16,2,16384]{2,1,0:T(2,128)(2,1)} broadcast(bf16[2,16384]{1,0:T(2,128)(2,1)} %param.8), dimensions={1,2} | broadcast | bytes 1114112 | tf_op jit(solution)/shard_map/broadcast_in_dim | solution.py:260
  3.3 7.9 %all-to-all-start = ((bf16[16,2,16384]{2,1,0:T(2,128)(2,1)}), bf16[16,2,16384]{2,1,0:T(2,128)(2,1)S(1)}, u32[]{:S(2)}, u32[]{:S(2)}) async-start(bf16[16,2,16384]{2,1,0:T(2,128)(2,1)} %broadcast_in_dim.4), calls=%async_computation | async-start | bytes 2097152 | tf_op jit(solution)/shard_map/all_to_all | solution.py:261
  11.2 13.3 %all-gather = bf16[8,4,8192]{2,1,0:T(4,128)(2,1)S(1)} all-gather(bf16[1,4,8192]{2,1,0:T(4,128)(2,1)} %bitcast.13), channel_id=1, replica_groups=mesh['src'=16,'tgt'=8] {'tgt'}, dimensions={0}, use_global_device_ids=true | all-gather | bytes 589824 | tf_op jit(solution)/shard_map/all_gather | solution.py:262
  24.5 0.1 reshape.12.source_ref.source_hbm
  24.6 1.8 %source_side.1.left_ref = bf16[8192,128]{1,0:T(8,128)(2,1)S(1)} custom-call(bf16[32,8192]{1,0:T(8,128)(2,1)S(1)} %reshape.12.source_ref.source_hbm), custom_call_target="tpu_custom_call" | custom-call | tf_op jit(solution)/shard_map/source_side/pallas_call | solution.py:267
  26.5 0.0 copy-start
  26.5 1.3 copy-done
  28.5 0.4 all-to-all-done
  28.9 0.4 reshape.10.target_ref.target_hbm
  29.3 0.0 copy-done.4
  29.3 0.0 copy-done.3
  29.3 0.0 copy-start.1
  29.3 1.6 %copy-done.1 = bf16[8192,128]{1,0:T(8,128)(2,1)S(1)} copy-done((bf16[8192,128]{1,0:T(8,128)(2,1)S(1)}, bf16[8192,128]{1,0:T(8,128)(2,1)}, u32[]{:S(2)}) %copy-start.1) | copy-done | bytes 2097176
  30.9 11.2 %row_sums.1 = (f32[1,8192]{1,0:T(1,128)S(1)}, bf16[16,512,512]{2,1,0:T(8,128)(2,1)S(1)}, bf16[16,512,512]{2,1,0:T(8,128)(2,1)S(1)}, bf16[16,512,512]{2,1,0:T(8,128)(2,1)S(1)}, bf16[16,512,512]{2,1,0:T(8,128)(2,1)S(1)}) custom-call(s32[2,64]{1,0:T(2,128)S(1)} %bitcast.9, s32[1,1]{1,0:T(1,128)S(6)} %copy.9.count_ref, bf16[8192,128]{1,0:T(8,128)(2,1)S(1)} %copy-done.1, ...), custom_call_target="tpu_custom_call" | custom-call | tf_op jit(solution)/shard_map/row_sums/pallas_call | solution.py:276
  42.2 17.9 %collective-permute-start = (f32[1,8192]{1,0:T(1,128)S(1)}, f32[1,8192]{1,0:T(1,128)S(1)}, u32[]{:S(2)}, u32[]{:S(2)}) collective-permute-start(f32[1,8192]{1,0:T(1,128)S(1)} %get-tuple-element.7), channel_id=1, source_target_pairs={{0,1},{1,0},{2,3},{3,2},{4,5},{5,4},{6,7},{7,6},{8,9},{9,8},{10,11... | collective-permute-start | bytes 98312 | tf_op jit(solution)/shard_map/ppermute | solution.py:255
  60.1 0.9 collective-permute-done
  61.0 0.1 multiply_add_fusion.1
  61.1 11.2 %collective-permute-start.1 = (f32[1,8192]{1,0:T(1,128)S(1)}, f32[1,8192]{1,0:T(1,128)S(1)}, u32[]{:S(2)}, u32[]{:S(2)}) collective-permute-start(f32[1,8192]{1,0:T(1,128)S(1)} %multiply_add_fusion.1), channel_id=1, source_target_pairs={{0,2},{1,3},{2,4},{3,5},{4,6},{5,7},{6,0},{7,1},{8,10},{9,11},{10,... | collective-permute-start | bytes 98312 | tf_op jit(solution)/shard_map/ppermute | solution.py:255
  72.3 0.0 collective-permute-start.2
  72.3 0.9 collective-permute-start.3
  73.3 0.0 copy-done.6
  73.3 0.6 collective-permute-done.1
  73.9 3.9 %collective-permute-done.2 = f32[1,8192]{1,0:T(1,128)S(1)} collective-permute-done((f32[1,8192]{1,0:T(1,128)S(1)}, f32[1,8192]{1,0:T(1,128)S(1)}, u32[]{:S(2)}, u32[]{:S(2)}) %collective-permute-start.2) | collective-permute-done | bytes 32800 | tf_op jit(solution)/shard_map/ppermute | solution.py:255
  77.8 0.0 collective-permute-done.3
  77.8 0.2 add_subtract_fusion.1.potential_ref
  78.1 0.0 copy-start.2
  78.1 0.0 copy-start.5
  78.1 8.6 %column_sums.1 = f32[1,16384]{1,0:T(1,128)S(1)} custom-call(s32[2,64]{1,0:T(2,128)S(1)} %bitcast.10, s32[1,1]{1,0:T(1,128)S(6)} %copy.9.count_ref, f32[1,8192]{1,0:T(1,128)S(1)} %add_subtract_fusion.1.potential_ref, bf16[16,512,512]{2,1,0:T(8,128)(2,1)S(1)} %get-tuple-element.8.store_0, bf16[16,512,512]{2,1,0:T(8,128)(2,1)S(1)} %get-tuple-element.9.store_1, ...), custom_call_target="tpu_custom_call" | custom-call | tf_op jit(solution)/shard_map/column_sums/pallas_call | solution.py:300
  86.7 0.0 copy-done.2
  86.7 10.5 %collective-permute-start.4 = (f32[1,16384]{1,0:T(1,128)S(1)}, f32[1,16384]{1,0:T(1,128)S(1)}, u32[]{:S(2)}, u32[]{:S(2)}) collective-permute-start(f32[1,16384]{1,0:T(1,128)S(1)} %column_sums.1), channel_id=1, source_target_pairs={{0,32},{8,40},{16,48},{24,56},{32,64},{40,72},{48,80},{56,88},{64,... | collective-permute-start | bytes 196616 | tf_op jit(solution)/shard_map/ppermute | solution.py:255
  97.2 0.0 collective-permute-start.5
  97.2 2.8 %collective-permute-start.6 = (f32[1,16384]{1,0:T(1,128)S(1)}, f32[1,16384]{1,0:T(1,128)S(1)}, u32[]{:S(2)}, u32[]{:S(2)}) collective-permute-start(f32[1,16384]{1,0:T(1,128)S(1)} %column_sums.1), channel_id=1, source_target_pairs={{0,96},{8,104},{16,112},{24,120},{32,0},{40,8},{48,16},{56,24},{64... | collective-permute-start | bytes 196616 | tf_op jit(solution)/shard_map/ppermute | solution.py:255
  100.0 0.0 collective-permute-done.4
  100.0 3.0 %collective-permute-done.5 = f32[1,16384]{1,0:T(1,128)S(1)} collective-permute-done((f32[1,16384]{1,0:T(1,128)S(1)}, f32[1,16384]{1,0:T(1,128)S(1)}, u32[]{:S(2)}, u32[]{:S(2)}) %collective-permute-start.5) | collective-permute-done | bytes 65568 | tf_op jit(solution)/shard_map/ppermute | solution.py:255
  103.0 0.0 collective-permute-done.6
  103.0 0.5 multiply_add_fusion
  103.4 0.1 collective-permute-start.7
  103.5 33.1 %collective-permute-start.8 = (f32[1,16384]{1,0:T(1,128)S(1)}, f32[1,16384]{1,0:T(1,128)S(1)}, u32[]{:S(2)}, u32[]{:S(2)}) collective-permute-start(f32[1,16384]{1,0:T(1,128)S(1)} %multiply_add_fusion), channel_id=1, source_target_pairs={{0,16},{8,24},{16,0},{24,8},{32,48},{40,56},{48,32},{56,40},{64,80... | collective-permute-start | bytes 196616 | tf_op jit(solution)/shard_map/ppermute | solution.py:255
  136.6 0.0 collective-permute-start.9
  136.6 0.0 copy-done.5
  136.6 1.0 collective-permute-done.7
  137.6 2.2 %collective-permute-done.8 = f32[1,16384]{1,0:T(1,128)S(1)} collective-permute-done((f32[1,16384]{1,0:T(1,128)S(1)}, f32[1,16384]{1,0:T(1,128)S(1)}, u32[]{:S(2)}, u32[]{:S(2)}) %collective-permute-start.8) | collective-permute-done | bytes 65568 | tf_op jit(solution)/shard_map/ppermute | solution.py:255
  139.7 1.1 collective-permute-done.9
  140.8 1.1 add_subtract_fusion
  (2 shorter events, 0.0 us)
Async XLA Ops:
  0.6 28.7 %copy-start.4 = (s32[1,1,2,64]{3,2,1,0:T(2,128)S(1)}, s32[1,1,2,64]{3,2,1,0:T(2,128)}, u32[]{:S(2)}) copy-start(s32[1,1,2,64]{3,2,1,0:T(2,128)} %param.12) | copy-start | bytes 1540
  0.6 28.7 %copy-start.3 = (f32[16384]{0:T(1024)S(1)}, f32[16384]{0:T(1024)}, u32[]{:S(2)}) copy-start(f32[16384]{0:T(1024)} %param.9) | copy-start | bytes 196612
  0.7 72.6 %copy-start.6 = (f32[8192]{0:T(1024)S(1)}, f32[8192]{0:T(1024)}, u32[]{:S(2)}) copy-start(f32[8192]{0:T(1024)} %param.10) | copy-start | bytes 98308
  3.3 25.6 %all-to-all-start = ((bf16[16,2,16384]{2,1,0:T(2,128)(2,1)}), bf16[16,2,16384]{2,1,0:T(2,128)(2,1)S(1)}, u32[]{:S(2)}, u32[]{:S(2)}) async-start(bf16[16,2,16384]{2,1,0:T(2,128)(2,1)} %broadcast_in_dim.4), calls=%async_computation | async-start | bytes 2097152 | tf_op jit(solution)/shard_map/all_to_all | solution.py:261
  26.5 1.3 copy-start
  29.3 1.6 %copy-start.1 = (bf16[8192,128]{1,0:T(8,128)(2,1)S(1)}, bf16[8192,128]{1,0:T(8,128)(2,1)}, u32[]{:S(2)}) copy-start(bf16[8192,128]{1,0:T(8,128)(2,1)} %copy-done) | copy-start | bytes 6291460
  42.2 18.8 %collective-permute-start = (f32[1,8192]{1,0:T(1,128)S(1)}, f32[1,8192]{1,0:T(1,128)S(1)}, u32[]{:S(2)}, u32[]{:S(2)}) collective-permute-start(f32[1,8192]{1,0:T(1,128)S(1)} %get-tuple-element.7), channel_id=1, source_target_pairs={{0,1},{1,0},{2,3},{3,2},{4,5},{5,4},{6,7},{7,6},{8,9},{9,8},{10,11... | collective-permute-start | bytes 98312 | tf_op jit(solution)/shard_map/ppermute | solution.py:255
  61.1 12.8 %collective-permute-start.1 = (f32[1,8192]{1,0:T(1,128)S(1)}, f32[1,8192]{1,0:T(1,128)S(1)}, u32[]{:S(2)}, u32[]{:S(2)}) collective-permute-start(f32[1,8192]{1,0:T(1,128)S(1)} %multiply_add_fusion.1), channel_id=1, source_target_pairs={{0,2},{1,3},{2,4},{3,5},{4,6},{5,7},{6,0},{7,1},{8,10},{9,11},{10,... | collective-permute-start | bytes 98312 | tf_op jit(solution)/shard_map/ppermute | solution.py:255
  72.3 5.5 %collective-permute-start.2 = (f32[1,8192]{1,0:T(1,128)S(1)}, f32[1,8192]{1,0:T(1,128)S(1)}, u32[]{:S(2)}, u32[]{:S(2)}) collective-permute-start(f32[1,8192]{1,0:T(1,128)S(1)} %multiply_add_fusion.1), channel_id=1, source_target_pairs={{0,4},{1,5},{2,6},{3,7},{4,0},{5,1},{6,2},{7,3},{8,12},{9,13},{10,... | collective-permute-start | bytes 98312 | tf_op jit(solution)/shard_map/ppermute | solution.py:255
  72.3 5.5 %collective-permute-start.3 = (f32[1,8192]{1,0:T(1,128)S(1)}, f32[1,8192]{1,0:T(1,128)S(1)}, u32[]{:S(2)}, u32[]{:S(2)}) collective-permute-start(f32[1,8192]{1,0:T(1,128)S(1)} %multiply_add_fusion.1), channel_id=1, source_target_pairs={{0,6},{1,7},{2,0},{3,1},{4,2},{5,3},{6,4},{7,5},{8,14},{9,15},{10,... | collective-permute-start | bytes 98312 | tf_op jit(solution)/shard_map/ppermute | solution.py:255
  78.1 8.6 %copy-start.2 = (f32[1,8192]{1,0:T(1,128)}, f32[1,8192]{1,0:T(1,128)S(1)}, u32[]{:S(2)}) copy-start(f32[1,8192]{1,0:T(1,128)S(1)} %add_subtract_fusion.1.potential_ref) | copy-start | bytes 98308
  78.1 58.5 %copy-start.5 = (f32[16384]{0:T(1024)S(1)}, f32[16384]{0:T(1024)}, u32[]{:S(2)}) copy-start(f32[16384]{0:T(1024)} %param.11) | copy-start | bytes 196612
  86.7 13.3 %collective-permute-start.4 = (f32[1,16384]{1,0:T(1,128)S(1)}, f32[1,16384]{1,0:T(1,128)S(1)}, u32[]{:S(2)}, u32[]{:S(2)}) collective-permute-start(f32[1,16384]{1,0:T(1,128)S(1)} %column_sums.1), channel_id=1, source_target_pairs={{0,32},{8,40},{16,48},{24,56},{32,64},{40,72},{48,80},{56,88},{64,... | collective-permute-start | bytes 196616 | tf_op jit(solution)/shard_map/ppermute | solution.py:255
  97.2 5.8 %collective-permute-start.5 = (f32[1,16384]{1,0:T(1,128)S(1)}, f32[1,16384]{1,0:T(1,128)S(1)}, u32[]{:S(2)}, u32[]{:S(2)}) collective-permute-start(f32[1,16384]{1,0:T(1,128)S(1)} %column_sums.1), channel_id=1, source_target_pairs={{0,64},{8,72},{16,80},{24,88},{32,96},{40,104},{48,112},{56,120},{... | collective-permute-start | bytes 196616 | tf_op jit(solution)/shard_map/ppermute | solution.py:255
  97.2 5.8 %collective-permute-start.6 = (f32[1,16384]{1,0:T(1,128)S(1)}, f32[1,16384]{1,0:T(1,128)S(1)}, u32[]{:S(2)}, u32[]{:S(2)}) collective-permute-start(f32[1,16384]{1,0:T(1,128)S(1)} %column_sums.1), channel_id=1, source_target_pairs={{0,96},{8,104},{16,112},{24,120},{32,0},{40,8},{48,16},{56,24},{64... | collective-permute-start | bytes 196616 | tf_op jit(solution)/shard_map/ppermute | solution.py:255
  103.4 34.1 %collective-permute-start.7 = (f32[1,16384]{1,0:T(1,128)S(1)}, f32[1,16384]{1,0:T(1,128)S(1)}, u32[]{:S(2)}, u32[]{:S(2)}) collective-permute-start(f32[1,16384]{1,0:T(1,128)S(1)} %multiply_add_fusion), channel_id=1, source_target_pairs={{0,8},{8,16},{16,24},{24,0},{32,40},{40,48},{48,56},{56,32},{64,72... | collective-permute-start | bytes 196616 | tf_op jit(solution)/shard_map/ppermute | solution.py:255
  103.5 36.2 %collective-permute-start.8 = (f32[1,16384]{1,0:T(1,128)S(1)}, f32[1,16384]{1,0:T(1,128)S(1)}, u32[]{:S(2)}, u32[]{:S(2)}) collective-permute-start(f32[1,16384]{1,0:T(1,128)S(1)} %multiply_add_fusion), channel_id=1, source_target_pairs={{0,16},{8,24},{16,0},{24,8},{32,48},{40,56},{48,32},{56,40},{64,80... | collective-permute-start | bytes 196616 | tf_op jit(solution)/shard_map/ppermute | solution.py:255
  136.6 4.3 %collective-permute-start.9 = (f32[1,16384]{1,0:T(1,128)S(1)}, f32[1,16384]{1,0:T(1,128)S(1)}, u32[]{:S(2)}, u32[]{:S(2)}) collective-permute-start(f32[1,16384]{1,0:T(1,128)S(1)} %multiply_add_fusion), channel_id=1, source_target_pairs={{0,24},{8,0},{16,8},{24,16},{32,56},{40,32},{48,40},{56,48},{64,88... | collective-permute-start | bytes 196616 | tf_op jit(solution)/shard_map/ppermute | solution.py:255

commit v4 on v3

--- a/solution.py
+++ b/solution.py
@@ -8,12 +8,14 @@
 from jax.sharding import PartitionSpec as P
 
 TILE = 512
+LINES = TILE // 128
 WIDTH = 32
 PIECES = 3
 LEFT = 128
 RIGHT = 112
 DEPTH = 48
-TOGETHER = 8
+TOGETHER = 16
+UNROLL = 4
 STORES = 4
 EPSILON = 0.1
 KAPPA = 1.4426950408889634 / EPSILON
@@ -26,10 +28,24 @@
 VMEM = pl.BlockSpec(memory_space=pltpu.VMEM)
 SMEM = pl.BlockSpec(memory_space=pltpu.SMEM)
 ANY = pl.BlockSpec(memory_space=pl.ANY)
+HBM = pl.BlockSpec(memory_space=pltpu.HBM)
 
 
 def at_tile(tile):
     return pl.ds(pl.multiple_of(tile * TILE, TILE), TILE)
+
+
+def write_line(ref, tile, line):
+    for part in range(LINES):
+        ref[pl.ds(tile * LINES + part, 1), :] = line[:, part * 128 : (part + 1) * 128]
+
+
+def read_line(ref, tile):
+    return jnp.concatenate([ref[pl.ds(tile * LINES + part, 1), :] for part in range(LINES)], axis=1)
+
+
+def highest_of(ref):
+    return jnp.max(jnp.max(ref[...], axis=0, keepdims=True), axis=1, keepdims=True)
 
 
 def pieces(value, number=PIECES):
@@ -44,8 +60,8 @@
     return jnp.sum(cells * cells, axis=0, keepdims=True)
 
 
-def general_lse(red_row, keep_row, list_ref, live, red_ref, keep_ref, bias_ref, out_ref, top, total):
-    keep_tiles = keep_ref.shape[1] // TILE
+def general_lse(red_row, keep_row, list_ref, live, read_red, read_keep, read_bias, out_ref, top, total):
+    keep_tiles = top.shape[1] // TILE
     half, scale = float(WIDTH), ALPHA
     rows_of = 64
 
@@ -56,14 +72,14 @@
         return 0
 
     def step(entry, _):
-        red_at = at_tile(list_ref[red_row, entry])
-        keep_at = at_tile(list_ref[keep_row, entry])
-        cells = red_ref[:, red_at].astype(F32)
-        terms = pieces(half * bias_ref[:, red_at] - 0.5 * squares(cells))
+        red_tile, keep_tile = list_ref[red_row, entry], list_ref[keep_row, entry]
+        keep_at = at_tile(keep_tile)
+        cells = read_red(red_tile)
+        terms = pieces(half * read_bias(red_tile) - 0.5 * squares(cells))
         filler = jnp.zeros((DEPTH - WIDTH - PIECES, TILE), F32)
         left = jnp.transpose(jnp.concatenate([cells] + terms + [filler, jnp.zeros((LEFT - DEPTH, TILE), F32)], axis=0))
         left = left.astype(BF16)[:, :DEPTH]
-        right = jnp.concatenate([keep_ref[:, keep_at].astype(F32), jnp.ones((PIECES, TILE), F32), filler], axis=0).astype(BF16)
+        right = jnp.concatenate([read_keep(keep_tile), jnp.ones((PIECES, TILE), F32), filler], axis=0).astype(BF16)
         highest, summed = top[:, keep_at], total[:, keep_at]
         for row in range(0, TILE, rows_of):
             z = jnp.dot(left[row : row + rows_of], right, preferred_element_type=F32)
@@ -80,12 +96,17 @@
         highest = jnp.max(top[:, at], axis=0, keepdims=True)
         summed = jnp.sum(total[:, at] * jnp.exp2(top[:, at] - highest), axis=0, keepdims=True)
         value = highest * (1.0 / KAPPA) + EPSILON * jnp.log(jnp.maximum(summed, 1.0))
-        out_ref[:, at] = value - squares(keep_ref[:, at].astype(F32)) * (0.5 / WIDTH)
+        write_line(out_ref, tile, value - squares(read_keep(tile)) * (0.5 / WIDTH))
         return 0
 
     lax.fori_loop(0, keep_tiles, clear, 0)
     lax.fori_loop(0, live, step, 0)
     lax.fori_loop(0, keep_tiles, finish, 0)
+
+
+def copies_kernel(part_ref, copies_ref):
+    for copy in range(copies_ref.shape[0]):
+        copies_ref[copy] = part_ref[...]
 
 
 def source_kernel(source_ref, left_ref):
@@ -97,7 +118,7 @@
         left_ref[at, :] = jnp.transpose(jnp.concatenate(rows, axis=0)).astype(BF16)
         return 0
 
-    lax.fori_loop(0, source_ref.shape[1] // TILE, prepare, 0)
+    lax.fori_loop(0, source_ref.shape[1] // TILE, prepare, 0, unroll=UNROLL)
 
 
 def groups(live, body):
@@ -116,20 +137,18 @@
 
 
 def row_kernel(
-    list_ref, count_ref, left_ref, target_ref, potential_ref, source_hbm,
+    list_ref, count_ref, left_hbm, target_ref, potential_ref, source_hbm,
     out_ref, store_0, store_1, store_2, store_3,
-    right, weight, sums, covered, smallest, top, total, source_ref, semaphore,
+    left_ref, right, weight, sums, covered, smallest, top, total, source_ref, semaphores,
 ):
     stores = (store_0, store_1, store_2, store_3)
     source_tiles = left_ref.shape[0] // TILE
-    target_tiles = target_ref.shape[1] // TILE
+    target_tiles = right.shape[1] // TILE
     live = count_ref[0, 0]
-    highest = jnp.max(potential_ref[...], axis=1, keepdims=True)
+    fetch = pltpu.make_async_copy(left_hbm, left_ref, semaphores.at[0])
+    fetch.start()
+    highest = highest_of(potential_ref)
     rows_of = 64
-
-    def clear(tile, _):
-        sums[at_tile(tile), :] = jnp.zeros((TILE, 128), F32)
-        return 0
 
     def prepare(tile, _):
         at = at_tile(tile)
@@ -139,12 +158,14 @@
         tail = pieces(squares(cells.astype(F32)) * -GAMMA) + [jnp.ones((PIECES, TILE), F32)]
         tail.append(jnp.zeros((RIGHT - PIECES * WIDTH - 2 * PIECES, TILE), F32))
         right[PIECES * WIDTH : RIGHT, at] = jnp.concatenate(tail, axis=0).astype(BF16)
-        weight[:, at] = jnp.exp2((potential_ref[:, at] - highest) * KAPPA)
+        weight[:, at] = jnp.exp2((read_line(potential_ref, tile) - highest) * KAPPA)
+        share = sums.shape[0] // target_tiles
+        sums[pl.ds(pl.multiple_of(tile * share, share), share), :] = jnp.zeros((share, 128), F32)
         return 0
 
     clear_marks(covered)
-    lax.fori_loop(0, source_tiles, clear, 0)
-    lax.fori_loop(0, target_tiles, prepare, 0)
+    lax.fori_loop(0, target_tiles, prepare, 0, unroll=UNROLL)
+    fetch.wait()
 
     def step(entry, store, slot):
         alive = (entry < live).astype(jnp.int32)
@@ -164,26 +185,31 @@
     smallest[...] = jnp.ones((1, TILE), F32)
 
     def finish(tile, _):
-        at = at_tile(tile)
         lines = sum(
             lax.dot_general(jnp.ones((16, 128), BF16), piece.astype(BF16), (((1,), (1,)), ((), ())), preferred_element_type=F32)
-            for piece in pieces(sums[at, :], 2)
+            for piece in pieces(sums[at_tile(tile), :], 2)
         )
         summed = lines[0:1]
         present = covered[tile] > 0
         value = highest + EPSILON * jnp.log(jnp.maximum(summed, TRUSTED))
-        out_ref[:, at] = jnp.where(present, value, LOWEST)
+        write_line(out_ref, tile, jnp.where(present, value, LOWEST))
         smallest[...] = jnp.minimum(smallest[...], jnp.where(present, summed, 1.0))
         return 0
 
-    lax.fori_loop(0, source_tiles, finish, 0)
+    lax.fori_loop(0, source_tiles, finish, 0, unroll=UNROLL)
 
     @pl.when(jnp.min(smallest[...]) < TRUSTED)
     def _():
-        copy = pltpu.make_async_copy(source_hbm, source_ref, semaphore)
+        copy = pltpu.make_async_copy(source_hbm, source_ref, semaphores.at[1])
         copy.start()
         copy.wait()
-        general_lse(1, 0, list_ref, live, target_ref, source_ref, potential_ref, out_ref, top, total)
+        general_lse(
+            1, 0, list_ref, live,
+            lambda tile: target_ref[:, at_tile(tile)].astype(F32),
+            lambda tile: source_ref[:, at_tile(tile)].astype(F32),
+            lambda tile: read_line(potential_ref, tile),
+            out_ref, top, total,
+        )
 
 
 def column_kernel(
@@ -193,14 +219,13 @@
 ):
     stores = (store_0, store_1, store_2, store_3)
     source_tiles = source_ref.shape[1] // TILE
-    target_tiles = target_ref.shape[1] // TILE
+    target_tiles = sums.shape[1] // TILE
     live = count_ref[0, 0]
-    highest = jnp.max(potential_ref[...], axis=1, keepdims=True)
+    highest = highest_of(potential_ref)
 
     def prepare(tile, _):
-        at = at_tile(tile)
-        terms = pieces(jnp.exp2((potential_ref[:, at] - highest) * KAPPA))
-        weight[:, at] = jnp.concatenate(terms + [jnp.zeros((16 - PIECES, TILE), F32)], axis=0).astype(BF16)
+        terms = pieces(jnp.exp2((read_line(potential_ref, tile) - highest) * KAPPA))
+        weight[:, at_tile(tile)] = jnp.concatenate(terms + [jnp.zeros((16 - PIECES, TILE), F32)], axis=0).astype(BF16)
         return 0
 
     def clear(tile, _):
@@ -208,8 +233,8 @@
         return 0
 
     clear_marks(covered)
-    lax.fori_loop(0, source_tiles, prepare, 0)
-    lax.fori_loop(0, target_tiles, clear, 0)
+    lax.fori_loop(0, source_tiles, prepare, 0, unroll=UNROLL)
+    lax.fori_loop(0, target_tiles, clear, 0, unroll=UNROLL)
 
     def step(entry, store, slot):
         alive = (entry < live).astype(jnp.int32)
@@ -222,15 +247,14 @@
     smallest[...] = jnp.ones((1, TILE), F32)
 
     def finish(tile, _):
-        at = at_tile(tile)
-        summed = jnp.sum(sums[:, at], axis=0, keepdims=True)
+        summed = jnp.sum(sums[:, at_tile(tile)], axis=0, keepdims=True)
         present = covered[tile] > 0
         value = highest + EPSILON * jnp.log(jnp.maximum(summed, TRUSTED))
-        out_ref[:, at] = jnp.where(present, value, LOWEST)
+        write_line(out_ref, tile, jnp.where(present, value, LOWEST))
         smallest[...] = jnp.minimum(smallest[...], jnp.where(present, summed, 1.0))
         return 0
 
-    lax.fori_loop(0, target_tiles, finish, 0)
+    lax.fori_loop(0, target_tiles, finish, 0, unroll=UNROLL)
 
     @pl.when(jnp.min(smallest[...]) < TRUSTED)
     def _():
@@ -238,7 +262,13 @@
             copy = pltpu.make_async_copy(hbm, ref, semaphore)
             copy.start()
             copy.wait()
-        general_lse(0, 1, list_ref, live, source_ref, target_ref, potential_ref, out_ref, top, total)
+        general_lse(
+            0, 1, list_ref, live,
+            lambda tile: source_ref[:, at_tile(tile)].astype(F32),
+            lambda tile: target_ref[:, at_tile(tile)].astype(F32),
+            lambda tile: read_line(potential_ref, tile),
+            out_ref, top, total,
+        )
 
 
 def merged(parts):
@@ -256,18 +286,31 @@
 
 
 def local(source_embed, target_embed, target_potential, log_source_mass, log_target_mass, tile_list, counts):
+    over_x = [along("src", 16, 4, 4, shift) for shift in (1, 2, 3)]
+    over_z = [along("src", 16, 4, 1, shift) for shift in (1, 2, 3)]
+    over_y = [along("tgt", 8, 4, 2, shift) for shift in (1, 2, 3)]
+    over_core = along("tgt", 8, 2, 1, 1)
+
     sources = lax.axis_size("src")
-    copies = jnp.broadcast_to(target_embed[None], (sources,) + target_embed.shape)
+    copies = pl.pallas_call(
+        copies_kernel,
+        name="target_copies",
+        out_shape=pltpu.VMEM((sources,) + target_embed.shape, BF16),
+        in_specs=[VMEM],
+        out_specs=VMEM,
+        compiler_params=pltpu.CompilerParams(vmem_limit_bytes=8 << 20),
+    )(target_embed)
     target_full = lax.all_to_all(copies, "src", 0, 0).reshape(WIDTH, -1)
     source_full = lax.all_gather(source_embed, "tgt", axis=0, tiled=True)
+
     own_list = tile_list[0, 0]
-    source_cells, target_cells = source_full.shape[1], target_full.shape[1]
+    source_cells, target_cells = source_embed.shape[1], target_embed.shape[1]
     slots = own_list.shape[1] // STORES
 
     left = pl.pallas_call(
         source_kernel,
         name="source_side",
-        out_shape=pltpu.VMEM((source_cells, LEFT), BF16),
+        out_shape=pltpu.HBM((source_cells, LEFT), BF16),
         in_specs=[VMEM],
         out_specs=VMEM,
         compiler_params=pltpu.CompilerParams(vmem_limit_bytes=10 << 20),
@@ -276,10 +319,12 @@
     row, *stores = pl.pallas_call(
         row_kernel,
         name="row_sums",
-        out_shape=(jax.ShapeDtypeStruct((1, source_cells), F32),) + (pltpu.VMEM((slots, TILE, TILE), BF16),) * STORES,
-        in_specs=[SMEM, SMEM, VMEM, VMEM, VMEM, ANY],
+        out_shape=(jax.ShapeDtypeStruct((source_cells // 128, 128), F32),)
+        + (pltpu.VMEM((slots, TILE, TILE), BF16),) * STORES,
+        in_specs=[SMEM, SMEM, HBM, VMEM, VMEM, ANY],
         out_specs=(VMEM,) * (1 + STORES),
         scratch_shapes=[
+            pltpu.VMEM((source_cells, LEFT), BF16),
             pltpu.VMEM((RIGHT, target_cells), BF16),
             pltpu.VMEM((1, target_cells), F32),
             pltpu.VMEM((source_cells, 128), F32),
@@ -288,19 +333,19 @@
             pltpu.VMEM((8, source_cells), F32),
             pltpu.VMEM((8, source_cells), F32),
             pltpu.VMEM((WIDTH, source_cells), BF16),
-            pltpu.SemaphoreType.DMA,
+            pltpu.SemaphoreType.DMA((2,)),
         ],
-        compiler_params=pltpu.CompilerParams(vmem_limit_bytes=12 << 20),
-    )(own_list, counts, left, target_full, target_potential[None], source_full)
-
-    row = merged([row, along("tgt", 8, 2, 1, 1)(row)])
-    row = merged([row] + [along("tgt", 8, 4, 2, shift)(row) for shift in (1, 2, 3)])
-    row_potential = EPSILON * log_source_mass[None] - row
+        compiler_params=pltpu.CompilerParams(vmem_limit_bytes=14 << 20),
+    )(own_list, counts, pltpu.with_memory_space_constraint(left, pltpu.HBM), target_full, target_potential.reshape(-1, 128), source_full)
+
+    row = merged([row, over_core(row)])
+    row = merged([row] + [send(row) for send in over_y])
+    row_potential = EPSILON * log_source_mass.reshape(-1, 128) - row
 
     column = pl.pallas_call(
         column_kernel,
         name="column_sums",
-        out_shape=jax.ShapeDtypeStruct((1, target_cells), F32),
+        out_shape=jax.ShapeDtypeStruct((target_cells // 128, 128), F32),
         in_specs=[SMEM, SMEM, VMEM] + [VMEM] * STORES + [ANY, ANY],
         out_specs=VMEM,
         scratch_shapes=[
@@ -317,10 +362,10 @@
         compiler_params=pltpu.CompilerParams(vmem_limit_bytes=10 << 20),
     )(own_list, counts, row_potential, *stores, source_full, target_full)
 
-    column = merged([column] + [along("src", 16, 4, 4, shift)(column) for shift in (1, 2, 3)])
-    column = merged([column] + [along("src", 16, 4, 1, shift)(column) for shift in (1, 2, 3)])
-    column_potential = EPSILON * log_target_mass[None] - column
-    return row_potential[0], column_potential[0]
+    column = merged([column] + [send(column) for send in over_x])
+    column = merged([column] + [send(column) for send in over_z])
+    column_potential = EPSILON * log_target_mass.reshape(-1, 128) - column
+    return row_potential.reshape(-1), column_potential.reshape(-1)
 
 
 def solution(mesh):

time: 144 us -> 136 us (0.944); the launches traced: 142 us -> 137 us
  starting transfers between devices: 84.4 us -> 68.5 us
  Pallas kernels: 21.7 us -> 35.9 us
  local copies, waits for them, and re-layouts: 6.13 us -> 1.42 us
  waiting for transfers between devices: 13.1 us -> 15.8 us
    pallas_call x1, Pallas kernels: 11.2 us -> 27.5 us  [local(): pl.pallas_call(row_kernel, name='row_sums', out_shape=(jax.ShapeDtypeStru...]
    ppermute x10, starting transfers between devices: 76.5 us -> 60.6 us  [along(): return lambda value: lax.ppermute(value, axis, pairs)]
    pallas_call x1, Pallas kernels: 8.6 us -> 5.07 us  [local(): pl.pallas_call(column_kernel, name='column_sums', out_shape=jax.ShapeDtyp...]
    broadcast_in_dim x1 -> x0, local copies, waits for them, and re-layouts: 2.65 us -> none  [local(): jnp.broadcast_to(target_embed[None], (sources,) + target_embed.shape)]
    unnamed x15 -> x13, local copies, waits for them, and re-layouts: 3.06 us -> 1 us
    ppermute x10, waiting for transfers between devices: 12.6 us -> 14.5 us  [along(): return lambda value: lax.ppermute(value, axis, pairs)]
    pallas_call x1 -> x2, Pallas kernels: 1.82 us -> 3.32 us  [the longest x1 2.28 us: local(): pl.pallas_call(source_kernel, name='source_side', out_shape=pltpu.HBM((so...]
  transfers between devices with their start and end apart: 11 -> 11, of which waited for: 8 -> 11; matrix products, arithmetic and copies ran while one was open for 0% -> 0% of each run, Pallas kernels for 1% -> 2%
where the time goes in v4:
time: 136 us; the launch traced here: 137 us
  starting transfers between devices  68.5 us (50%)
  Pallas kernels  35.9 us (26%)
  waiting for transfers between devices  15.8 us (12%)
  blocking collectives  13.3 us (10%)
  local copies, waits for them, and re-layouts  1.42 us (1%)
  between operations  1.39 us (1%)
    ppermute x10, starting transfers between devices, along(): return lambda value: lax.ppermute(value, axis, pairs)  60.6 us
    pallas_call x1, Pallas kernels, local(): pl.pallas_call(row_kernel, name='row_sums', out_shape=(jax.ShapeDtypeStru...  27.5 us
    ppermute x10, waiting for transfers between devices, along(): return lambda value: lax.ppermute(value, axis, pairs)  14.5 us
    all_gather x1, blocking collectives, local(): source_full = lax.all_gather(source_embed, 'tgt', axis=0, tiled=True)  13.3 us
    all_to_all x1, starting transfers between devices, local(): target_full = lax.all_to_all(copies, 'src', 0, 0).reshape(WIDTH, -1)  7.88 us
    pallas_call x1, Pallas kernels, local(): pl.pallas_call(column_kernel, name='column_sums', out_shape=jax.ShapeDtyp...  5.07 us
  transfers between devices with their start and end apart: 11, of which 11 were waited for; matrix products, arithmetic and copies ran while one was open for 0% of the time, Pallas kernels for 2%

profile of v4, /device:TPU:24, one launch (start us, length us, event | category | flops | bytes accessed | tf_op | source)
XLA Modules:
  0.0 137.1 jit_solution(7996071054186504421)
XLA Ops:
  0.6 0.0 copy-start.1
  0.6 0.0 copy-start.2
  0.7 0.9 copy-done.2
  1.5 0.0 copy-start.3
  1.5 0.0 copy-start.5
  1.5 1.0 target_copies.1
  2.6 7.9 %all-to-all-start = ((bf16[16,2,16384]{2,1,0:T(2,128)(2,1)}), bf16[16,2,16384]{2,1,0:T(2,128)(2,1)S(1)}, u32[]{:S(2)}, u32[]{:S(2)}) async-start(bf16[16,2,16384]{2,1,0:T(2,128)(2,1)} %target_copies.1), calls=%async_computation | async-start | bytes 2097152 | tf_op jit(solution)/shard_map/all_to_all | solution.py:303
  11.1 13.3 %all-gather = bf16[8,4,8192]{2,1,0:T(4,128)(2,1)S(1)} all-gather(bf16[1,4,8192]{2,1,0:T(4,128)(2,1)} %bitcast.16), channel_id=1, replica_groups=mesh['src'=16,'tgt'=8] {'tgt'}, dimensions={0}, use_global_device_ids=true | all-gather | bytes 589824 | tf_op jit(solution)/shard_map/all_gather | solution.py:304
  24.4 0.1 reshape.27.source_ref.source_hbm
  24.5 2.3 %source_side.1.left_hbm = bf16[8192,128]{1,0:T(8,128)(2,1)} custom-call(bf16[32,8192]{1,0:T(8,128)(2,1)S(1)} %reshape.27.source_ref.source_hbm), custom_call_target="tpu_custom_call" | custom-call | tf_op jit(solution)/shard_map/source_side/pallas_call | solution.py:310
  26.8 1.3 all-to-all-done
  28.1 0.4 reshape.22.target_ref.target_hbm
  28.6 0.0 copy-done.1
  28.6 0.0 copy-done.3
  28.6 27.5 %row_sums.1 = (f32[64,128]{1,0:T(8,128)S(1)}, bf16[16,512,512]{2,1,0:T(8,128)(2,1)S(1)}, bf16[16,512,512]{2,1,0:T(8,128)(2,1)S(1)}, bf16[16,512,512]{2,1,0:T(8,128)(2,1)S(1)}, bf16[16,512,512]{2,1,0:T(8,128)(2,1)S(1)}) custom-call(s32[2,64]{1,0:T(2,128)S(1)} %bitcast.14, s32[1,1]{1,0:T(1,128)S(6)} %copy.9.count_ref, bf16[8192,128]{1,0:T(8,128)(2,1)} %source_side.1.left_hbm, ...), custom_call_target="tpu_custom_call" | custom-call | tf_op jit(solution)/shard_map/row_sums/pallas_call | solution.py:319
  56.1 4.8 %collective-permute-start = (f32[64,128]{1,0:T(8,128)S(1)}, f32[64,128]{1,0:T(8,128)S(1)}, u32[]{:S(2)}, u32[]{:S(2)}) collective-permute-start(f32[64,128]{1,0:T(8,128)S(1)} %get-tuple-element.7), channel_id=1, source_target_pairs={{0,1},{1,0},{2,3},{3,2},{4,5},{5,4},{6,7},{7,6},{8,9},{9,8},{10,11... | collective-permute-start | bytes 98312 | tf_op jit(solution)/shard_map/ppermute | solution.py:285
  60.9 0.9 collective-permute-done
  61.7 0.7 collective-permute-start.3
  62.5 0.0 collective-permute-start.2
  62.5 2.8 %collective-permute-start.1 = (f32[64,128]{1,0:T(8,128)S(1)}, f32[64,128]{1,0:T(8,128)S(1)}, u32[]{:S(2)}, u32[]{:S(2)}) collective-permute-start(f32[64,128]{1,0:T(8,128)S(1)} %multiply_add_fusion.1), channel_id=1, source_target_pairs={{0,2},{1,3},{2,4},{3,5},{4,6},{5,7},{6,0},{7,1},{8,10},{9,11},{10,... | collective-permute-start | bytes 98312 | tf_op jit(solution)/shard_map/ppermute | solution.py:285
  65.2 1.9 %collective-permute-done.3 = f32[64,128]{1,0:T(8,128)S(1)} collective-permute-done((f32[64,128]{1,0:T(8,128)S(1)}, f32[64,128]{1,0:T(8,128)S(1)}, u32[]{:S(2)}, u32[]{:S(2)}) %collective-permute-start.3) | collective-permute-done | bytes 32800 | tf_op jit(solution)/shard_map/ppermute | solution.py:285
  67.2 0.7 collective-permute-done.2
  67.9 0.3 collective-permute-done.1
  68.2 0.0 copy-done.5
  68.2 0.0 copy-start
  68.2 0.0 copy-start.4
  68.2 5.1 %column_sums.1 = f32[128,128]{1,0:T(8,128)S(1)} custom-call(s32[2,64]{1,0:T(2,128)S(1)} %bitcast.15, s32[1,1]{1,0:T(1,128)S(6)} %copy.9.count_ref, f32[64,128]{1,0:T(8,128)S(1)} %bitcast_subtract_fusion.1.potential_ref, bf16[16,512,512]{2,1,0:T(8,128)(2,1)S(1)} %get-tuple-element.8.store_0, bf16[16,512,512]{2,1,0:T(8,128)(2,1)S(1)} %get-tuple-element.9.store_1, ...), custom_call_target="tpu_custom_call" | custom-call | tf_op jit(solution)/shard_map/column_sums/pallas_call | solution.py:345
  73.3 0.0 copy-done
  73.3 15.7 %collective-permute-start.6 = (f32[128,128]{1,0:T(8,128)S(1)}, f32[128,128]{1,0:T(8,128)S(1)}, u32[]{:S(2)}, u32[]{:S(2)}) collective-permute-start(f32[128,128]{1,0:T(8,128)S(1)} %column_sums.1), channel_id=1, source_target_pairs={{0,96},{8,104},{16,112},{24,120},{32,0},{40,8},{48,16},{56,24},{64... | collective-permute-start | bytes 196616 | tf_op jit(solution)/shard_map/ppermute | solution.py:285
  89.0 15.8 %collective-permute-start.5 = (f32[128,128]{1,0:T(8,128)S(1)}, f32[128,128]{1,0:T(8,128)S(1)}, u32[]{:S(2)}, u32[]{:S(2)}) collective-permute-start(f32[128,128]{1,0:T(8,128)S(1)} %column_sums.1), channel_id=1, source_target_pairs={{0,64},{8,72},{16,80},{24,88},{32,96},{40,104},{48,112},{56,120},{... | collective-permute-start | bytes 196616 | tf_op jit(solution)/shard_map/ppermute | solution.py:285
  104.9 0.0 collective-permute-start.4
  104.9 0.2 collective-permute-done.6
  105.1 2.1 %collective-permute-done.5 = f32[128,128]{1,0:T(8,128)S(1)} collective-permute-done((f32[128,128]{1,0:T(8,128)S(1)}, f32[128,128]{1,0:T(8,128)S(1)}, u32[]{:S(2)}, u32[]{:S(2)}) %collective-permute-start.5) | collective-permute-done | bytes 65568 | tf_op jit(solution)/shard_map/ppermute | solution.py:285
  107.1 3.2 %collective-permute-done.4 = f32[128,128]{1,0:T(8,128)S(1)} collective-permute-done((f32[128,128]{1,0:T(8,128)S(1)}, f32[128,128]{1,0:T(8,128)S(1)}, u32[]{:S(2)}, u32[]{:S(2)}) %collective-permute-start.4) | collective-permute-done | bytes 65568 | tf_op jit(solution)/shard_map/ppermute | solution.py:285
  110.4 0.1 multiply_add_fusion
  110.4 19.8 %collective-permute-start.9 = (f32[128,128]{1,0:T(8,128)S(1)}, f32[128,128]{1,0:T(8,128)S(1)}, u32[]{:S(2)}, u32[]{:S(2)}) collective-permute-start(f32[128,128]{1,0:T(8,128)S(1)} %multiply_add_fusion), channel_id=1, source_target_pairs={{0,24},{8,0},{16,8},{24,16},{32,56},{40,32},{48,40},{56,48},{64,88... | collective-permute-start | bytes 196616 | tf_op jit(solution)/shard_map/ppermute | solution.py:285
  130.2 0.0 collective-permute-start.8
  130.2 0.9 collective-permute-start.7
  131.2 1.6 %collective-permute-done.9 = f32[128,128]{1,0:T(8,128)S(1)} collective-permute-done((f32[128,128]{1,0:T(8,128)S(1)}, f32[128,128]{1,0:T(8,128)S(1)}, u32[]{:S(2)}, u32[]{:S(2)}) %collective-permute-start.9) | collective-permute-done | bytes 65568 | tf_op jit(solution)/shard_map/ppermute | solution.py:285
  132.7 3.4 %collective-permute-done.8 = f32[128,128]{1,0:T(8,128)S(1)} collective-permute-done((f32[128,128]{1,0:T(8,128)S(1)}, f32[128,128]{1,0:T(8,128)S(1)}, u32[]{:S(2)}, u32[]{:S(2)}) %collective-permute-start.8) | collective-permute-done | bytes 65568 | tf_op jit(solution)/shard_map/ppermute | solution.py:285
  136.1 0.3 collective-permute-done.7
  136.4 0.0 copy-done.4
  136.4 0.7 fusion
  (2 shorter events, 0.1 us)
Async XLA Ops:
  0.6 27.9 %copy-start.1 = (f32[16384]{0:T(1024)S(1)}, f32[16384]{0:T(1024)}, u32[]{:S(2)}) copy-start(f32[16384]{0:T(1024)} %param.9) | copy-start | bytes 196612
  0.6 0.9 copy-start.2
  1.5 27.1 %copy-start.3 = (s32[1,1,2,64]{3,2,1,0:T(2,128)S(1)}, s32[1,1,2,64]{3,2,1,0:T(2,128)}, u32[]{:S(2)}) copy-start(s32[1,1,2,64]{3,2,1,0:T(2,128)} %param.12) | copy-start | bytes 1540
  1.5 66.6 %copy-start.5 = (f32[8192]{0:T(1024)S(1)}, f32[8192]{0:T(1024)}, u32[]{:S(2)}) copy-start(f32[8192]{0:T(1024)} %param.10) | copy-start | bytes 98308
  2.6 25.6 %all-to-all-start = ((bf16[16,2,16384]{2,1,0:T(2,128)(2,1)}), bf16[16,2,16384]{2,1,0:T(2,128)(2,1)S(1)}, u32[]{:S(2)}, u32[]{:S(2)}) async-start(bf16[16,2,16384]{2,1,0:T(2,128)(2,1)} %target_copies.1), calls=%async_computation | async-start | bytes 2097152 | tf_op jit(solution)/shard_map/all_to_all | solution.py:303
  56.1 5.7 %collective-permute-start = (f32[64,128]{1,0:T(8,128)S(1)}, f32[64,128]{1,0:T(8,128)S(1)}, u32[]{:S(2)}, u32[]{:S(2)}) collective-permute-start(f32[64,128]{1,0:T(8,128)S(1)} %get-tuple-element.7), channel_id=1, source_target_pairs={{0,1},{1,0},{2,3},{3,2},{4,5},{5,4},{6,7},{7,6},{8,9},{9,8},{10,11... | collective-permute-start | bytes 98312 | tf_op jit(solution)/shard_map/ppermute | solution.py:285
  61.7 5.4 %collective-permute-start.3 = (f32[64,128]{1,0:T(8,128)S(1)}, f32[64,128]{1,0:T(8,128)S(1)}, u32[]{:S(2)}, u32[]{:S(2)}) collective-permute-start(f32[64,128]{1,0:T(8,128)S(1)} %multiply_add_fusion.1), channel_id=1, source_target_pairs={{0,6},{1,7},{2,0},{3,1},{4,2},{5,3},{6,4},{7,5},{8,14},{9,15},{10,... | collective-permute-start | bytes 98312 | tf_op jit(solution)/shard_map/ppermute | solution.py:285
  62.5 5.4 %collective-permute-start.2 = (f32[64,128]{1,0:T(8,128)S(1)}, f32[64,128]{1,0:T(8,128)S(1)}, u32[]{:S(2)}, u32[]{:S(2)}) collective-permute-start(f32[64,128]{1,0:T(8,128)S(1)} %multiply_add_fusion.1), channel_id=1, source_target_pairs={{0,4},{1,5},{2,6},{3,7},{4,0},{5,1},{6,2},{7,3},{8,12},{9,13},{10,... | collective-permute-start | bytes 98312 | tf_op jit(solution)/shard_map/ppermute | solution.py:285
  62.5 5.7 %collective-permute-start.1 = (f32[64,128]{1,0:T(8,128)S(1)}, f32[64,128]{1,0:T(8,128)S(1)}, u32[]{:S(2)}, u32[]{:S(2)}) collective-permute-start(f32[64,128]{1,0:T(8,128)S(1)} %multiply_add_fusion.1), channel_id=1, source_target_pairs={{0,2},{1,3},{2,4},{3,5},{4,6},{5,7},{6,0},{7,1},{8,10},{9,11},{10,... | collective-permute-start | bytes 98312 | tf_op jit(solution)/shard_map/ppermute | solution.py:285
  68.2 5.1 %copy-start = (f32[64,128]{1,0:T(8,128)}, f32[64,128]{1,0:T(8,128)S(1)}, u32[]{:S(2)}) copy-start(f32[64,128]{1,0:T(8,128)S(1)} %bitcast_subtract_fusion.1.potential_ref) | copy-start | bytes 98308
  68.2 68.2 %copy-start.4 = (f32[16384]{0:T(1024)S(1)}, f32[16384]{0:T(1024)}, u32[]{:S(2)}) copy-start(f32[16384]{0:T(1024)} %param.11) | copy-start | bytes 196612
  73.3 31.7 %collective-permute-start.6 = (f32[128,128]{1,0:T(8,128)S(1)}, f32[128,128]{1,0:T(8,128)S(1)}, u32[]{:S(2)}, u32[]{:S(2)}) collective-permute-start(f32[128,128]{1,0:T(8,128)S(1)} %column_sums.1), channel_id=1, source_target_pairs={{0,96},{8,104},{16,112},{24,120},{32,0},{40,8},{48,16},{56,24},{64... | collective-permute-start | bytes 196616 | tf_op jit(solution)/shard_map/ppermute | solution.py:285
  89.0 18.1 %collective-permute-start.5 = (f32[128,128]{1,0:T(8,128)S(1)}, f32[128,128]{1,0:T(8,128)S(1)}, u32[]{:S(2)}, u32[]{:S(2)}) collective-permute-start(f32[128,128]{1,0:T(8,128)S(1)} %column_sums.1), channel_id=1, source_target_pairs={{0,64},{8,72},{16,80},{24,88},{32,96},{40,104},{48,112},{56,120},{... | collective-permute-start | bytes 196616 | tf_op jit(solution)/shard_map/ppermute | solution.py:285
  104.9 5.5 %collective-permute-start.4 = (f32[128,128]{1,0:T(8,128)S(1)}, f32[128,128]{1,0:T(8,128)S(1)}, u32[]{:S(2)}, u32[]{:S(2)}) collective-permute-start(f32[128,128]{1,0:T(8,128)S(1)} %column_sums.1), channel_id=1, source_target_pairs={{0,32},{8,40},{16,48},{24,56},{32,64},{40,72},{48,80},{56,88},{64,... | collective-permute-start | bytes 196616 | tf_op jit(solution)/shard_map/ppermute | solution.py:285
  110.4 22.3 %collective-permute-start.9 = (f32[128,128]{1,0:T(8,128)S(1)}, f32[128,128]{1,0:T(8,128)S(1)}, u32[]{:S(2)}, u32[]{:S(2)}) collective-permute-start(f32[128,128]{1,0:T(8,128)S(1)} %multiply_add_fusion), channel_id=1, source_target_pairs={{0,24},{8,0},{16,8},{24,16},{32,56},{40,32},{48,40},{56,48},{64,88... | collective-permute-start | bytes 196616 | tf_op jit(solution)/shard_map/ppermute | solution.py:285
  130.2 5.9 %collective-permute-start.8 = (f32[128,128]{1,0:T(8,128)S(1)}, f32[128,128]{1,0:T(8,128)S(1)}, u32[]{:S(2)}, u32[]{:S(2)}) collective-permute-start(f32[128,128]{1,0:T(8,128)S(1)} %multiply_add_fusion), channel_id=1, source_target_pairs={{0,16},{8,24},{16,0},{24,8},{32,48},{40,56},{48,32},{56,40},{64,80... | collective-permute-start | bytes 196616 | tf_op jit(solution)/shard_map/ppermute | solution.py:285
  130.2 6.2 %collective-permute-start.7 = (f32[128,128]{1,0:T(8,128)S(1)}, f32[128,128]{1,0:T(8,128)S(1)}, u32[]{:S(2)}, u32[]{:S(2)}) collective-permute-start(f32[128,128]{1,0:T(8,128)S(1)} %multiply_add_fusion), channel_id=1, source_target_pairs={{0,8},{8,16},{16,24},{24,0},{32,40},{40,48},{48,56},{56,32},{64,72... | collective-permute-start | bytes 196616 | tf_op jit(solution)/shard_map/ppermute | solution.py:285
